TPU v7x, 32 devices: a whole 2x2x4 slice. The times are simulated.
32 devices in a mesh: ctx: 4 (over y, core), exp: 8 (over z, x).
Axes of the slice: x: 2, y: 2, z: 4, core: 2. Of those that a mesh axis runs over, the one named last changes fastest.
Arguments:
- tokens: bfloat16 [8, 1024, 1024], P('exp', 'ctx'), may hold values from -6 to 6
- segments: int32 [8, 1024], P('exp'), may hold values from 0 to 2, as said below
- routes: int32 [8, 1024, 8], P('exp', 'ctx'), may hold values from 0 to 31, all different within a row
- gain_attn: bfloat16 [1024], P(('ctx', 'exp')), may hold values from 0.5 to 1.5
- gain_moe: bfloat16 [1024], P(('ctx', 'exp')), may hold values from 0.5 to 1.5
- query_weight: bfloat16 [1024, 1024], P(('ctx', 'exp')), may hold values from -0.375 to 0.375
- key_weight: bfloat16 [1024, 512], P(('ctx', 'exp')), may hold values from -0.1875 to 0.1875
- value_weight: bfloat16 [1024, 512], P(('ctx', 'exp')), may hold values from -0.1875 to 0.1875
- w_output: bfloat16 [1024, 1024], P(('ctx', 'exp')), may hold values from -0.75 to 0.75
- w_router: bfloat16 [1024, 32], P(('ctx', 'exp')), may hold values from -0.09375 to 0.09375
- w_expert_in: bfloat16 [32, 1024, 1024], P('exp', 'ctx'), may hold values from -0.1875 to 0.1875
- w_expert_out: bfloat16 [32, 512, 1024], P('exp', 'ctx'), may hold values from -0.5 to 0.5
- cotangent: bfloat16 [8, 1024, 1024], P('exp', 'ctx'), may hold values from -6 to 6
Outputs:
- mixed_out: bfloat16 [8, 1024, 1024], P('exp', 'ctx')
- grad_tokens: float32 [8, 1024, 1024], P('exp', 'ctx')
- grad_gain_attn: float32 [1024], P(('ctx', 'exp'))
- grad_gain_moe: float32 [1024], P(('ctx', 'exp'))
- grad_w_query: float32 [1024, 1024], P(('ctx', 'exp'))
- grad_w_key: float32 [1024, 512], P(('ctx', 'exp'))
- grad_w_value: float32 [1024, 512], P(('ctx', 'exp'))
- grad_w_output: float32 [1024, 1024], P(('ctx', 'exp'))
- grad_w_router: float32 [1024, 32], P(('ctx', 'exp'))
- grad_w_expert_in: float32 [32, 1024, 1024], P('exp', 'ctx')
- grad_w_expert_out: float32 [32, 512, 1024], P('exp', 'ctx')
Inputs may be any that keep to these rules, and one draw needn't show every extreme that they name: `routes`: each position names 8 different experts, and every expert is named somewhere. `segments`: in every pack the numbers never fall; document 0 ends within the first 256 positions, document 2 begins within the last 256 positions, document 1 lies between.
All inputs are finite; a program needn't handle non-finite values.
Results may differ from a plain program's by a relative error of at most 0.022.
Values may be sent and summed in bfloat16 or wider, within the bound.
A program may use at most 256 MiB of HBM per device.

v0:
```python
import math

import jax
import jax.numpy as jnp
from jax import lax
from jax.sharding import PartitionSpec as P

QUERY_HEADS = 16
KEY_VALUE_HEADS = 8
HEAD_SIZE = 64
EXPERTS = 32
TOPK = 8
FF = 512
CAP = 72


EPSILON = 1e-06
MASK_FILLER = -1e30


def rms_scale(values):
    return lax.rsqrt(jnp.mean(values * values, -1, keepdims=True) + EPSILON)


def inner_rows(left, right):
    return lax.dot_general(
        left, right, (((0,), (0,)), ((), ())), preferred_element_type=jnp.float32
    )


def outer_cols(left, right):
    return lax.dot_general(
        left, right, (((1,), (1,)), ((), ())), preferred_element_type=jnp.float32
    )


def allowed_block(query_pos, query_seg, seg_all, offset, key_total_count):
    key_pos = offset + jnp.arange(key_total_count, dtype=jnp.int32)
    key_seg = lax.dynamic_slice_in_dim(seg_all, offset, key_total_count)
    return (key_pos[None, :] <= query_pos[:, None]) & (key_seg[None, :] == query_seg[:, None])


def head_scores(heads_of_queries, key_segment_slice, factor):
    key_total_count = key_segment_slice.shape[0]
    heads_of_keys = key_segment_slice.reshape(key_total_count, KEY_VALUE_HEADS, -1)
    return (
        jnp.einsum(
            "ihgd,jhd->hgij", heads_of_queries, heads_of_keys, preferred_element_type=jnp.float32
        )
        * factor
    )


def slot_tables(pair_ids):
    pair_count = pair_ids.shape[0]
    member = (pair_ids[:, None] == jnp.arange(EXPERTS, dtype=jnp.int32)[None, :]).astype(jnp.int32)
    earlier = jnp.cumsum(member, 0) - member
    slot_place = jnp.sum(earlier * member, 1, dtype=jnp.int32)
    is_kept = slot_place < CAP
    slot_index = jnp.where(is_kept, pair_ids * CAP + slot_place, EXPERTS * CAP)
    slot_filler = (
        jnp.full((EXPERTS * CAP,), -1, jnp.int32)
        .at[slot_index]
        .set(jnp.arange(pair_count, dtype=jnp.int32), mode="drop")
    )
    return (slot_index, is_kept, slot_filler)


def local(
    tokens,
    segments,
    routes,
    gain_attn,
    gain_moe,
    query_weight,
    key_weight,
    value_weight,
    w_output,
    w_router,
    w_expert_in,
    w_expert_out,
    cotangent,
):
    shards = lax.axis_size("ctx")
    groups = lax.axis_size("exp")
    ctx_rank = lax.axis_index("ctx")
    gain_one, gain_two, full_query, full_key, full_value, full_output, full_router = (
        lax.all_gather(gain_attn, ("ctx", "exp"), axis=0, tiled=True),
        lax.all_gather(gain_moe, ("ctx", "exp"), axis=0, tiled=True),
        lax.all_gather(query_weight, ("ctx", "exp"), axis=0, tiled=True),
        lax.all_gather(key_weight, ("ctx", "exp"), axis=0, tiled=True),
        lax.all_gather(value_weight, ("ctx", "exp"), axis=0, tiled=True),
        lax.all_gather(w_output, ("ctx", "exp"), axis=0, tiled=True),
        lax.all_gather(w_router, ("ctx", "exp"), axis=0, tiled=True),
    )
    expert_in, expert_out = (
        lax.all_gather(w_expert_in, "ctx", axis=1, tiled=True),
        lax.all_gather(w_expert_out, "ctx", axis=1, tiled=True),
    )
    inputs = tokens[0].astype(jnp.float32)
    token_rows = inputs.shape[0]
    seq_len = token_rows * shards
    head_cluster = QUERY_HEADS // KEY_VALUE_HEADS
    factor = 1.0 / math.sqrt(HEAD_SIZE)
    kv_width = key_weight.shape[1]
    seg_all = segments[0]
    query_pos = ctx_rank * token_rows + jnp.arange(token_rows, dtype=jnp.int32)
    query_seg = lax.dynamic_slice_in_dim(seg_all, ctx_rank * token_rows, token_rows)
    scale_one = rms_scale(inputs)
    gain_one_f = gain_one.astype(jnp.float32)
    normalized_input = (inputs * scale_one * gain_one_f).astype(jnp.bfloat16)
    query_matrix = jnp.dot(normalized_input, full_query, preferred_element_type=jnp.float32).astype(
        jnp.bfloat16
    )
    key_rows = jnp.dot(normalized_input, full_key, preferred_element_type=jnp.float32).astype(
        jnp.bfloat16
    )
    value_rows = jnp.dot(normalized_input, full_value, preferred_element_type=jnp.float32).astype(
        jnp.bfloat16
    )
    heads_of_queries = query_matrix.reshape(token_rows, KEY_VALUE_HEADS, head_cluster, HEAD_SIZE)
    group_size = math.gcd(shards, max(1, 1024 // token_rows))
    key_range_width = group_size * token_rows
    turns_needed = ctx_rank // group_size + 1
    running_maximum = jnp.full(
        (KEY_VALUE_HEADS, head_cluster, token_rows), MASK_FILLER, jnp.float32
    )
    key_segment_slice = lax.all_gather(key_rows, "ctx", axis=0, tiled=True)
    value_segment_slice = lax.all_gather(value_rows, "ctx", axis=0, tiled=True)
    key_total_count = key_segment_slice.shape[0]
    scores = head_scores(heads_of_queries, key_segment_slice, factor)
    allowed = allowed_block(query_pos, query_seg, seg_all, jnp.int32(0), key_total_count)
    scores = jnp.where(allowed, scores, MASK_FILLER)
    new_max = jnp.maximum(running_maximum, jnp.max(scores, -1))
    weights = jnp.where(allowed, jnp.exp(scores - new_max[..., None]), 0.0)
    run_sum = jnp.sum(weights, -1)
    heads_of_values = value_segment_slice.reshape(key_total_count, KEY_VALUE_HEADS, HEAD_SIZE)
    run_acc = jnp.einsum(
        "hgij,jhd->ihgd",
        weights.astype(jnp.bfloat16),
        heads_of_values,
        preferred_element_type=jnp.float32,
    )
    running_maximum, run_sum, run_acc = (new_max, run_sum, run_acc)
    log_norm = running_maximum + jnp.log(run_sum)
    heads_out = run_acc / jnp.transpose(run_sum, (2, 0, 1))[..., None]
    attn_low = heads_out.reshape(token_rows, -1).astype(jnp.bfloat16)
    resid = inputs + jnp.dot(attn_low, full_output, preferred_element_type=jnp.float32)
    scale_two = rms_scale(resid)
    gain_two_f = gain_two.astype(jnp.float32)
    moe_in = (resid * scale_two * gain_two_f).astype(jnp.bfloat16)
    logits = jnp.dot(moe_in, full_router, preferred_element_type=jnp.float32)
    route_ids = routes[0]
    one_hot = (route_ids[:, :, None] == jnp.arange(EXPERTS, dtype=jnp.int32)[None, None, :]).astype(
        jnp.float32
    )
    chosen = jnp.sum(one_hot * logits[:, None, :], -1)
    gates = jax.nn.softmax(chosen, axis=-1)
    slot_index, is_kept, slot_filler = slot_tables(route_ids.reshape(-1))
    filled = slot_filler >= 0
    token_of = jnp.maximum(slot_filler, 0) // TOPK
    local_experts = EXPERTS // groups
    send_rows = jnp.where(
        filled[:, None], jnp.take(moe_in, token_of, axis=0), jnp.zeros((), jnp.bfloat16)
    )
    send_rows = send_rows.reshape(groups, local_experts, CAP, -1)
    received = lax.all_to_all(send_rows, "exp", split_axis=0, concat_axis=0, tiled=True)
    pre = jnp.einsum("sjcd,jdf->sjcf", received, expert_in, preferred_element_type=jnp.float32)
    gate_part = pre[..., :FF]
    up_part = pre[..., FF:]
    hidden = (jax.nn.silu(gate_part) * up_part).astype(jnp.bfloat16)
    expert_rows = jnp.einsum(
        "sjcf,jfd->sjcd", hidden, expert_out, preferred_element_type=jnp.float32
    ).astype(jnp.bfloat16)
    returned = lax.all_to_all(expert_rows, "exp", split_axis=0, concat_axis=0, tiled=True).reshape(
        EXPERTS * CAP, -1
    )
    safe_slot = jnp.minimum(slot_index, EXPERTS * CAP - 1)
    picked = jnp.where(
        is_kept[:, None], jnp.take(returned, safe_slot, axis=0), jnp.zeros((), jnp.bfloat16)
    )
    picked = picked.astype(jnp.float32).reshape(token_rows, TOPK, -1)
    branch = jnp.sum(gates[:, :, None] * picked, 1)
    mixed_out = (resid + branch).astype(jnp.bfloat16)
    grad_out = cotangent[0].astype(jnp.float32)
    grad_picked = jnp.sum(grad_out[:, None, :] * picked, -1)
    grad_chosen = gates * (grad_picked - jnp.sum(gates * grad_picked, -1, keepdims=True))
    grad_logits = jnp.sum(one_hot * grad_chosen[:, :, None], 1)
    slot_gate = jnp.where(filled, jnp.take(gates.reshape(-1), jnp.maximum(slot_filler, 0)), 0.0)
    grad_send = (slot_gate[:, None] * jnp.take(grad_out, token_of, axis=0)).astype(jnp.bfloat16)
    grad_send = grad_send.reshape(groups, local_experts, CAP, -1)
    grad_rows = lax.all_to_all(grad_send, "exp", split_axis=0, concat_axis=0, tiled=True)
    grad_hidden = jnp.einsum(
        "sjcd,jfd->sjcf", grad_rows, expert_out, preferred_element_type=jnp.float32
    )
    sigmoid_gate = jax.nn.sigmoid(gate_part)
    grad_gate = grad_hidden * up_part * sigmoid_gate * (1.0 + gate_part * (1.0 - sigmoid_gate))
    grad_up = grad_hidden * gate_part * sigmoid_gate
    grad_pre = jnp.concatenate([grad_gate, grad_up], -1).astype(jnp.bfloat16)
    grad_expert_out = jnp.einsum(
        "sjcf,sjcd->jfd", hidden, grad_rows, preferred_element_type=jnp.float32
    )
    grad_expert_in = jnp.einsum(
        "sjcd,sjcf->jdf", received, grad_pre, preferred_element_type=jnp.float32
    )
    grad_received = jnp.einsum(
        "sjcf,jdf->sjcd", grad_pre, expert_in, preferred_element_type=jnp.float32
    ).astype(jnp.bfloat16)
    grad_back = lax.all_to_all(
        grad_received, "exp", split_axis=0, concat_axis=0, tiled=True
    ).reshape(EXPERTS * CAP, -1)
    grad_pairs = jnp.where(
        is_kept[:, None], jnp.take(grad_back, safe_slot, axis=0), jnp.zeros((), jnp.bfloat16)
    )
    grad_pairs = grad_pairs.astype(jnp.float32).reshape(token_rows, TOPK, -1)
    grad_moe_in = (
        jnp.sum(grad_pairs, 1)
        + outer_cols(grad_logits.astype(jnp.bfloat16), full_router) * 0.0
        + lax.dot_general(
            grad_logits,
            full_router.astype(jnp.float32),
            (((1,), (1,)), ((), ())),
            precision=lax.Precision.HIGHEST,
            preferred_element_type=jnp.float32,
        )
    )
    grad_router = lax.dot_general(
        moe_in.astype(jnp.float32),
        grad_logits,
        (((0,), (0,)), ((), ())),
        precision=lax.Precision.HIGHEST,
        preferred_element_type=jnp.float32,
    )
    weighted_two = grad_moe_in * gain_two_f
    grad_gain_two = jnp.sum(grad_moe_in * resid * scale_two, 0)
    cube_two = scale_two * scale_two * scale_two
    grad_resid = (
        grad_out
        + scale_two * weighted_two
        - resid * cube_two * jnp.mean(weighted_two * resid, -1, keepdims=True)
    )
    grad_resid_low = grad_resid.astype(jnp.bfloat16)
    grad_output_w = inner_rows(attn_low, grad_resid_low)
    grad_heads = (
        outer_cols(grad_resid_low, full_output)
        .astype(jnp.bfloat16)
        .reshape(token_rows, KEY_VALUE_HEADS, head_cluster, HEAD_SIZE)
    )
    delta = jnp.transpose(jnp.sum(grad_heads.astype(jnp.float32) * heads_out, -1), (1, 2, 0))
    all_keys, all_values = (
        lax.all_gather(key_rows, "ctx", axis=0, tiled=True),
        lax.all_gather(value_rows, "ctx", axis=0, tiled=True),
    )

    def block_grads(offset):
        key_segment_slice = lax.dynamic_slice_in_dim(all_keys, offset, key_range_width)
        value_segment_slice = lax.dynamic_slice_in_dim(all_values, offset, key_range_width)
        scores = head_scores(heads_of_queries, key_segment_slice, factor)
        allowed = allowed_block(query_pos, query_seg, seg_all, offset, key_range_width)
        probs_full = jnp.where(allowed, jnp.exp(scores - log_norm[..., None]), 0.0)
        heads_of_keys = key_segment_slice.reshape(key_range_width, KEY_VALUE_HEADS, HEAD_SIZE)
        heads_of_values = value_segment_slice.reshape(key_range_width, KEY_VALUE_HEADS, HEAD_SIZE)
        grad_probs = jnp.einsum(
            "ihgd,jhd->hgij", grad_heads, heads_of_values, preferred_element_type=jnp.float32
        )
        grad_scores = (probs_full * (grad_probs - delta[..., None])).astype(jnp.bfloat16)
        query_part = jnp.einsum(
            "hgij,jhd->ihgd", grad_scores, heads_of_keys, preferred_element_type=jnp.float32
        )
        return (probs_full, grad_scores, query_part)

    query_begin_index = jnp.zeros(
        (token_rows, KEY_VALUE_HEADS, head_cluster, HEAD_SIZE), jnp.float32
    )

    def back_turn(turn, running):
        grad_query_acc, key_grad_buf = running
        offset = turn * key_range_width
        probs_full, grad_scores, query_part = block_grads(offset)
        grad_key_part = (
            jnp.einsum(
                "hgij,ihgd->jhd", grad_scores, heads_of_queries, preferred_element_type=jnp.float32
            )
            * factor
        )
        grad_value_part = jnp.einsum(
            "hgij,ihgd->jhd",
            probs_full.astype(jnp.bfloat16),
            grad_heads,
            preferred_element_type=jnp.float32,
        )
        joined = jnp.concatenate(
            [
                grad_key_part.reshape(key_range_width, -1),
                grad_value_part.reshape(key_range_width, -1),
            ],
            1,
        )
        key_grad_buf = lax.dynamic_update_slice_in_dim(key_grad_buf, joined, offset, 0)
        return (grad_query_acc + query_part, key_grad_buf)

    back_start = (query_begin_index, jnp.zeros((seq_len, 2 * kv_width), jnp.float32))
    grad_query_acc, key_grad_buf = lax.fori_loop(0, turns_needed, back_turn, back_start)
    own_grads = lax.psum_scatter(
        key_grad_buf.astype(jnp.bfloat16), "ctx", scatter_dimension=0, tiled=True
    ).astype(jnp.float32)
    grad_keys = own_grads[:, :kv_width].astype(jnp.bfloat16)
    grad_values = own_grads[:, kv_width:].astype(jnp.bfloat16)
    grad_query = (grad_query_acc * factor).reshape(token_rows, -1).astype(jnp.bfloat16)
    grad_query_w = inner_rows(normalized_input, grad_query)
    grad_key_w = inner_rows(normalized_input, grad_keys)
    grad_value_w = inner_rows(normalized_input, grad_values)
    grad_normed = (
        outer_cols(grad_query, full_query)
        + outer_cols(grad_keys, full_key)
        + outer_cols(grad_values, full_value)
    )
    weighted_one = grad_normed * gain_one_f
    grad_gain_one = jnp.sum(grad_normed * inputs * scale_one, 0)
    cube_one = scale_one * scale_one * scale_one
    grad_inputs = (
        grad_resid
        + scale_one * weighted_one
        - inputs * cube_one * jnp.mean(weighted_one * inputs, -1, keepdims=True)
    )
    dense_sums = (
        lax.psum_scatter(grad_gain_one, ("ctx", "exp"), scatter_dimension=0, tiled=True),
        lax.psum_scatter(grad_gain_two, ("ctx", "exp"), scatter_dimension=0, tiled=True),
        lax.psum_scatter(grad_query_w, ("ctx", "exp"), scatter_dimension=0, tiled=True),
        lax.psum_scatter(grad_key_w, ("ctx", "exp"), scatter_dimension=0, tiled=True),
        lax.psum_scatter(grad_value_w, ("ctx", "exp"), scatter_dimension=0, tiled=True),
        lax.psum_scatter(grad_output_w, ("ctx", "exp"), scatter_dimension=0, tiled=True),
        lax.psum_scatter(grad_router, ("ctx", "exp"), scatter_dimension=0, tiled=True),
    )
    expert_sums = (
        lax.psum_scatter(
            grad_expert_in.astype(jnp.bfloat16), "ctx", scatter_dimension=1, tiled=True
        ).astype(jnp.float32),
        lax.psum_scatter(
            grad_expert_out.astype(jnp.bfloat16), "ctx", scatter_dimension=1, tiled=True
        ).astype(jnp.float32),
    )
    return (mixed_out[None], grad_inputs[None]) + tuple(dense_sums) + tuple(expert_sums)


def solution(mesh):
    return jax.shard_map(
        local,
        mesh=mesh,
        in_specs=(
            P("exp", "ctx", None),
            P("exp", None),
            P("exp", "ctx", None),
            P(("ctx", "exp")),
            P(("ctx", "exp")),
            P(("ctx", "exp"), None),
            P(("ctx", "exp"), None),
            P(("ctx", "exp"), None),
            P(("ctx", "exp"), None),
            P(("ctx", "exp"), None),
            P("exp", "ctx", None),
            P("exp", "ctx", None),
            P("exp", "ctx", None),
        ),
        out_specs=(
            P("exp", "ctx", None),
            P("exp", "ctx", None),
            P(("ctx", "exp")),
            P(("ctx", "exp")),
            P(("ctx", "exp"), None),
            P(("ctx", "exp"), None),
            P(("ctx", "exp"), None),
            P(("ctx", "exp"), None),
            P(("ctx", "exp"), None),
            P("exp", "ctx", None),
            P("exp", "ctx", None),
        ),
        check_vma=False,
    )
```

profile of v0, /device:TPU:0, one launch (start us, length us, event | category | flops | bytes accessed | tf_op | source)
XLA Modules:
  0.0 1795.1 jit_solution(6531178815053596219)
XLA Ops:
  10.4 42.0 %all-reduce.5 = (bf16[1024]{0:T(1024)(128)(2,1)S(1)}, bf16[1024]{0:T(1024)(128)(2,1)S(1)}) all-reduce(bf16[1024]{0:T(1024)(128)(2,1)S(1)} %dynamic-update-slice, bf16[1024]{0:T(1024)(128)(2,1)S(1)} %dynamic-update-slice.1), channel_id=1, replica_groups=mesh['ctx'=4,'exp'=8] {'ctx','exp'}, use_global_device_ids=true, to_apply=%add | all-reduce | flops 2048 | bytes 8192
  54.3 13.2 all-gather.13.cloned.1.call-done
  70.2 53.1 %all-gather.9.cloned.1.call-done = bf16[1024,512]{1,0:T(8,128)(2,1)} async-done(((bf16[32,512]{1,0:T(8,128)(2,1)}), bf16[1024,512]{1,0:T(8,128)(2,1)}) %all-gather.9.cloned.1.call-update) | async-done | bytes 1048592 | tf_op jit(solution)/shard_map/all_gather | solution.py:92
  128.2 9.1 reduce-window.6
  138.4 8.3 scatter_custom_fusion
  148.8 11.1 all-gather.11.cloned.1.call-done
  161.4 57.9 %all-gather.17.cloned.1.call-done = bf16[1024,1024]{1,0:T(8,128)(2,1)} async-done(((bf16[32,1024]{1,0:T(8,128)(2,1)}), bf16[1024,1024]{1,0:T(8,128)(2,1)}) %all-gather.17.cloned.1.call-update) | async-done | bytes 2097168 | tf_op jit(solution)/shard_map/all_gather | solution.py:90
  226.3 4.0 fusion.14
  230.3 4.6 fusion.109
  234.9 42.6 %all-gather.19.cloned.1.call-done = bf16[1024,1024]{1,0:T(8,128)(2,1)} async-done(((bf16[32,1024]{1,0:T(8,128)(2,1)}), bf16[1024,1024]{1,0:T(8,128)(2,1)}) %all-gather.19.cloned.1.call-update) | async-done | bytes 2097168 | tf_op jit(solution)/shard_map/all_gather | solution.py:93
  280.1 8.2 gather_fusion
  288.3 6.3 select_select_fusion
  294.6 4.6 all-to-all-start
  300.0 104.4 %all-to-all-done = bf16[8,4,72,1024]{3,2,1,0:T(8,128)(2,1)} async-done(((bf16[8,4,72,1024]{3,2,1,0:T(8,128)(2,1)}), bf16[8,4,72,1024]{3,2,1,0:T(8,128)(2,1)}, u32[]{:S(2)}, u32[]{:S(2)}) %all-to-all-start) | async-done | bytes 4718624 | tf_op jit(solution)/shard_map/all_to_all | solution.py:167
  404.3 8.9 fusion.40
  413.2 3.6 copy-done.11
  419.6 5.5 convert_bitcast_fusion.2
  427.7 4.8 all-to-all-start.1
  432.6 8.2 gather_fusion.2
  440.9 152.5 %all_gather.43 = bf16[1024,32]{1,0:T(8,128)(2,1)S(1)} all-gather(bf16[32,32]{1,0:T(8,128)(2,1)S(1)} %copy-done.33), channel_id=1, replica_groups=mesh['ctx'=4,'exp'=8] {'ctx','exp'}, dimensions={0}, use_global_device_ids=true | all-gather | bytes 67584 | tf_op jit(solution)/shard_map/all_gather | solution.py:94
  593.8 13.9 gather_fusion.3
  611.7 12.3 gather_fusion.1
  624.2 4.7 multiply_convert_fusion
  628.9 105.3 %all_to_all.20 = bf16[8,4,72,1024]{3,2,1,0:T(8,128)(2,1)S(1)} all-to-all(bf16[8,4,72,1024]{3,2,1,0:T(8,128)(2,1)S(1)} %multiply_convert_fusion), channel_id=1, replica_groups=mesh['ctx'=4,'exp'=8] {'exp'}, dimensions={0} | all-to-all | bytes 9437184 | tf_op jit(solution)/shard_map/all_to_all | solution.py:192
  734.2 10.5 fusion.28
  744.7 9.2 convert_bitcast_fusion.1
  756.8 4.6 all-to-all-start.3
  761.6 102.8 %all-to-all-done.3 = bf16[8,4,72,1024]{3,2,1,0:T(8,128)(2,1)} async-done(((bf16[8,4,72,1024]{3,2,1,0:T(8,128)(2,1)}), bf16[8,4,72,1024]{3,2,1,0:T(8,128)(2,1)}, u32[]{:S(2)}, u32[]{:S(2)}) %all-to-all-start.3) | async-done | bytes 4718624 | tf_op jit(solution)/shard_map/all_to_all | solution.py:209
  864.4 14.0 gather_fusion.4
  878.3 13.0 convert_reduce_fusion
  899.6 38.1 %while.13 = (s32[]{:T(128)}, f32[256,8,2,64]{0,3,2,1:T(8,128)S(1)}, bf16[1024,1024]{0,1:T(8,128)(2,1)}, s32[]{:T(128)}, s32[1024]{0:T(1024)S(1)}, /*index=5*/s32...) while((s32[]{:T(128)}, f32[256,8,2,64]{0,3,2,1:T(8,128)S(1)}, ...), condition=%wide.region_19.21_spmd.clone, body=%wide.region_18.20_spmd.clone.sunk | while | flops 2732590336 | bytes 123534520 | solution.py:303
  899.9 8.1 fusion.172
  908.3 9.1 fusion.173
  917.5 3.7 bitcast_multiply_fusion.4
  921.2 8.5 fusion.175
  932.8 5.0 fusion.174
  938.1 8.7 bitcast_convert_fusion.1
  946.9 11.3 bitcast_convert_fusion
  960.9 6.8 reduce-scatter.9.cloned.1.call-done
  982.2 33.1 %reduce-scatter.23.cloned.1.call-done = bf16[4,128,1024]{2,1,0:T(8,128)(2,1)} async-done(((bf16[4,512,1024]{2,1,0:T(8,128)(2,1)}), bf16[4,128,1024]{2,1,0:T(8,128)(2,1)}) %reduce-scatter.23.cloned.1.call-update) | async-done | bytes 1048592 | tf_op jit(solution)/shard_map/reduce_scatter | solution.py:339
  1020.8 39.7 %all-reduce.4 = (f32[1024]{0:T(1024)S(1)}, f32[1024]{0:T(1024)S(1)}) all-reduce(f32[1024]{0:T(1024)S(1)} %get-tuple-element.165, f32[1024]{0:T(1024)S(1)} %copy-done.32), channel_id=3, replica_groups=mesh['ctx'=4,'exp'=8] {'ctx','exp'}, use_global_device_ids=true, to_apply=%region_23.25.clone | all-reduce | flops 2048 | bytes 16384
  1063.0 27.5 %reduce-scatter.21.cloned.1.call-done = bf16[4,256,1024]{2,1,0:T(8,128)(2,1)} async-done(((bf16[4,1024,1024]{2,1,0:T(8,128)(2,1)}), bf16[4,256,1024]{2,1,0:T(8,128)(2,1)}) %reduce-scatter.21.cloned.1.call-update) | async-done | bytes 2097168 | tf_op jit(solution)/shard_map/reduce_scatter | solution.py:336
  1090.4 4.1 convert_element_type.169
  1094.5 132.7 %reduce-scatter.19.cloned.1.call-done = f32[32,32]{1,0:T(8,128)} async-done(((f32[1024,32]{1,0:T(8,128)}), f32[32,32]{1,0:T(8,128)}) %reduce-scatter.19.cloned.1.call-update) | async-done | bytes 4112 | tf_op jit(solution)/shard_map/reduce_scatter | solution.py:333
  1227.2 137.1 %reduce-scatter.13.cloned.1.call-done = f32[32,512]{1,0:T(8,128)} async-done(((f32[1024,512]{1,0:T(8,128)}), f32[32,512]{1,0:T(8,128)}) %reduce-scatter.13.cloned.1.call-update) | async-done | bytes 65552 | tf_op jit(solution)/shard_map/reduce_scatter | solution.py:330
  1364.3 137.0 %reduce-scatter.15.cloned.1.call-done = f32[32,512]{1,0:T(8,128)} async-done(((f32[1024,512]{1,0:T(8,128)}), f32[32,512]{1,0:T(8,128)}) %reduce-scatter.15.cloned.1.call-update) | async-done | bytes 65552 | tf_op jit(solution)/shard_map/reduce_scatter | solution.py:331
  1501.3 143.4 %reduce-scatter.17.cloned.1.call-done = f32[32,1024]{1,0:T(8,128)} async-done(((f32[1024,1024]{1,0:T(8,128)}), f32[32,1024]{1,0:T(8,128)}) %reduce-scatter.17.cloned.1.call-update) | async-done | bytes 131088 | tf_op jit(solution)/shard_map/reduce_scatter | solution.py:332
  1644.7 143.3 %reduce-scatter.11.cloned.1.call-done = f32[32,1024]{1,0:T(8,128)} async-done(((f32[1024,1024]{1,0:T(8,128)}), f32[32,1024]{1,0:T(8,128)}) %reduce-scatter.11.cloned.1.call-update) | async-done | bytes 131088 | tf_op jit(solution)/shard_map/reduce_scatter | solution.py:329
  (199 shorter events, 77.1 us)
Async XLA Ops:
  7.2 120.6 %copy-start.27 = (s32[1,256,8]{1,2,0:T(8,128)S(1)}, s32[1,256,8]{1,2,0:T(8,128)}, u32[]{:S(2)}) copy-start(s32[1,256,8]{1,2,0:T(8,128)} %param.19) | copy-start | bytes 24580
  7.2 60.3 %all-gather.13.cloned.1.call-start = ((), (), s32[]{:S(2)}) async-start(), calls=%async_computation.14 | async-start | bytes 1081344 | tf_op jit(solution)/shard_map/all_gather | solution.py:91
  7.9 115.4 %all-gather.9.cloned.1.call-start = ((), (), s32[]{:S(2)}) async-start(), calls=%async_computation.12 | async-start | bytes 1081344 | tf_op jit(solution)/shard_map/all_gather | solution.py:92
  8.7 138.6 %all-gather.15.cloned.1.call-start = ((), (), s32[]{:S(2)}) async-start(), calls=%async_computation.15 | async-start | bytes 1310720 | tf_op jit(solution)/shard_map/all_gather | solution.py:128
  52.5 166.8 %copy-start.25 = (f32[1024]{0:T(1024)}, f32[1024]{0:T(1024)S(1)}, u32[]{:S(2)}) copy-start(f32[1024]{0:T(1024)S(1)} %convert_element_type.136) | copy-start | bytes 12292
  54.3 165.0 %copy-start.30 = (f32[256]{0:T(256)}, f32[256]{0:T(256)S(1)}, u32[]{:S(2)}) copy-start(f32[256]{0:T(256)S(1)} %get-tuple-element.211) | copy-start | bytes 3076
  70.1 76.8 %copy-start.23 = (s32[1,1024]{1,0:T(1,128)S(1)}, s32[1,1024]{1,0:T(1,128)}, u32[]{:S(2)}) copy-start(s32[1,1024]{1,0:T(1,128)} %param.18) | copy-start | bytes 12292
  70.1 89.8 %all-gather.11.cloned.1.call-start = ((), (), s32[]{:S(2)}) async-start(), calls=%async_computation.13 | async-start | bytes 1310720 | tf_op jit(solution)/shard_map/all_gather | solution.py:129
  125.9 93.4 %all-gather.17.cloned.1.call-start = ((), (), s32[]{:S(2)}) async-start(), calls=%async_computation.16 | async-start | bytes 2162688 | tf_op jit(solution)/shard_map/all_gather | solution.py:90
  126.5 151.0 %all-gather.19.cloned.1.call-start = ((), (), s32[]{:S(2)}) async-start(), calls=%async_computation.17 | async-start | bytes 2162688 | tf_op jit(solution)/shard_map/all_gather | solution.py:93
  127.1 92.2 %copy-start.7 = (bf16[1,256,1024]{2,1,0:T(8,128)(2,1)S(1)}, bf16[1,256,1024]{2,1,0:T(8,128)(2,1)}, u32[]{:S(2)}) copy-start(bf16[1,256,1024]{2,1,0:T(8,128)(2,1)} %param.17) | copy-start | bytes 1572868
  127.1 277.3 %all-gather.21.cloned.1.call-start = ((), (), s32[]{:S(2)}) async-start(), calls=%async_computation.18 | async-start | bytes 10485760 | tf_op jit(solution)/shard_map/all_gather | solution.py:97
  147.0 76.7 %copy-start.28 = (s32[1,256]{1,0:T(1,128)}, s32[1,256]{1,0:T(1,128)S(1)}, u32[]{:S(2)}) copy-start(s32[1,256]{1,0:T(1,128)S(1)} %constant_dynamic-slice_fusion) | copy-start | bytes 3076
  148.8 77.4 %copy-start.2 = (bf16[1024,512]{0,1:T(8,128)(2,1)}, bf16[1024,512]{0,1:T(8,128)(2,1)S(1)}, u32[]{:S(2)}) copy-start(bf16[1024,512]{0,1:T(8,128)(2,1)S(1)} %copy.88) | copy-start | bytes 3145732
  161.4 68.9 %copy-start.20 = (bf16[1024,512]{0,1:T(8,128)(2,1)}, bf16[1024,512]{0,1:T(8,128)(2,1)S(1)}, u32[]{:S(2)}) copy-start(bf16[1024,512]{0,1:T(8,128)(2,1)S(1)} %copy.87) | copy-start | bytes 3145732
  234.9 45.0 %copy-start.16 = (bf16[256,8,2,64]{0,3,2,1:T(8,128)(2,1)}, bf16[256,8,2,64]{0,3,2,1:T(8,128)(2,1)S(1)}, u32[]{:S(2)}) copy-start(bf16[256,8,2,64]{0,3,2,1:T(8,128)(2,1)S(1)} %get-tuple-element.216) | copy-start | bytes 1572868
  280.1 313.3 %copy-start = (bf16[256,1024]{1,0:T(8,128)(2,1)}, bf16[256,1024]{1,0:T(8,128)(2,1)S(1)}, u32[]{:S(2)}) copy-start(bf16[256,1024]{1,0:T(8,128)(2,1)S(1)} %multiply_convert_fusion.3) | copy-start | bytes 1572868
  294.6 109.7 %all-to-all-start = ((bf16[8,4,72,1024]{3,2,1,0:T(8,128)(2,1)}), bf16[8,4,72,1024]{3,2,1,0:T(8,128)(2,1)}, u32[]{:S(2)}, u32[]{:S(2)}) async-start(bf16[8,4,72,1024]{3,2,1,0:T(8,128)(2,1)} %select_select_fusion), calls=%async_computation | async-start | bytes 9437184 | tf_op jit(solution)/shard_map/all_to_all | solution.py:167
  299.2 120.4 %all-gather.23.cloned.1.call-start = ((), (), s32[]{:S(2)}) async-start(), calls=%async_computation.19 | async-start | bytes 5242880 | tf_op jit(solution)/shard_map/all_gather | solution.py:98
  427.7 4.8 copy-start.14
  427.7 166.0 %all-to-all-start.1 = ((bf16[8,4,72,1024]{3,2,1,0:T(8,128)(2,1)}), bf16[8,4,72,1024]{3,2,1,0:T(8,128)(2,1)}, u32[]{:S(2)}, u32[]{:S(2)}) async-start(bf16[8,4,72,1024]{3,2,1,0:T(8,128)(2,1)} %copy.98), calls=%async_computation.1 | async-start | bytes 9437184 | tf_op jit(solution)/shard_map/all_to_all | solution.py:175
  432.6 8.3 copy-start.33
  734.2 10.5 copy-start.13
  744.7 9.2 copy-start.35
  756.8 107.5 %all-to-all-start.3 = ((bf16[8,4,72,1024]{3,2,1,0:T(8,128)(2,1)}), bf16[8,4,72,1024]{3,2,1,0:T(8,128)(2,1)}, u32[]{:S(2)}, u32[]{:S(2)}) async-start(bf16[8,4,72,1024]{3,2,1,0:T(8,128)(2,1)} %copy.101), calls=%async_computation.3 | async-start | bytes 9437184 | tf_op jit(solution)/shard_map/all_to_all | solution.py:209
  761.4 206.2 %reduce-scatter.9.cloned.1.call-start = ((), (), s32[]{:S(2)}) async-start(), calls=%async_computation.20 | async-start | bytes 2621440 | tf_op jit(solution)/shard_map/reduce_scatter | solution.py:304
  761.6 130.1 %copy-start.21 = (f32[256,32]{0,1:T(8,128)}, f32[256,32]{0,1:T(8,128)S(1)}, u32[]{:S(2)}) copy-start(f32[256,32]{0,1:T(8,128)S(1)} %select_reduce_fusion) | copy-start | bytes 98308
  895.5 4.1 copy-start.3
  895.5 4.1 copy-start.6
  895.5 4.1 copy-start.24
  895.5 4.1 copy-start.29
  937.8 9.1 copy-start.36
  937.8 77.5 %reduce-scatter.23.cloned.1.call-start = ((), (), s32[]{:S(2)}) async-start(), calls=%async_computation.27 | async-start | bytes 5242880 | tf_op jit(solution)/shard_map/reduce_scatter | solution.py:339
  946.8 143.6 %reduce-scatter.21.cloned.1.call-start = ((), (), s32[]{:S(2)}) async-start(), calls=%async_computation.26 | async-start | bytes 10485760 | tf_op jit(solution)/shard_map/reduce_scatter | solution.py:336
  958.2 9.5 copy-start.8
  958.2 9.5 copy-start.26
  958.2 9.4 copy-start.31
  958.3 269.0 %reduce-scatter.19.cloned.1.call-start = ((), (), s32[]{:S(2)}) async-start(), calls=%async_computation.25 | async-start | bytes 540672 | tf_op jit(solution)/shard_map/reduce_scatter | solution.py:333
  960.8 12.8 copy-start.10
  960.8 12.8 copy-start.17
  960.8 403.5 %reduce-scatter.13.cloned.1.call-start = ((), (), s32[]{:S(2)}) async-start(), calls=%async_computation.22 | async-start | bytes 2162688 | tf_op jit(solution)/shard_map/reduce_scatter | solution.py:330
  970.6 530.8 %reduce-scatter.15.cloned.1.call-start = ((), (), s32[]{:S(2)}) async-start(), calls=%async_computation.23 | async-start | bytes 2162688 | tf_op jit(solution)/shard_map/reduce_scatter | solution.py:331
  973.5 671.2 %reduce-scatter.17.cloned.1.call-start = ((), (), s32[]{:S(2)}) async-start(), calls=%async_computation.24 | async-start | bytes 4325376 | tf_op jit(solution)/shard_map/reduce_scatter | solution.py:332
  976.3 811.8 %reduce-scatter.11.cloned.1.call-start = ((), (), s32[]{:S(2)}) async-start(), calls=%async_computation.21 | async-start | bytes 4325376 | tf_op jit(solution)/shard_map/reduce_scatter | solution.py:329
  982.2 37.8 %copy-start.18 = (bf16[256,1024]{0,1:T(8,128)(2,1)S(1)}, bf16[256,1024]{0,1:T(8,128)(2,1)}, u32[]{:S(2)}) copy-start(bf16[256,1024]{0,1:T(8,128)(2,1)} %reduce-scatter.9.cloned.1.call-done) | copy-start | bytes 1572868
  982.2 38.6 %copy-start.32 = (f32[1024]{0:T(1024)S(1)}, f32[1024]{0:T(1024)}, u32[]{:S(2)}) copy-start(f32[1024]{0:T(1024)} %get-tuple-element.163) | copy-start | bytes 12292
  982.2 79.5 %copy-start.34 = (f32[256]{0:T(256)S(1)}, f32[256]{0:T(256)}, u32[]{:S(2)}) copy-start(f32[256]{0:T(256)} %get-tuple-element.210) | copy-start | bytes 3076
  1015.3 4.7 copy-start.19
  (8 other events, 18.8 us)
Sparse Core Ops, SparseCore 0:
  11.0 56.4 all-gather.12
  70.5 52.7 all-gather.8
  125.4 15.6 all-gather.14
  143.1 16.7 all-gather.10
  162.7 56.4 all-gather.16
  222.1 55.3 all-gather.18
  279.1 57.1 all-gather.20
  337.8 34.4 all-gather.22
  937.9 29.7 reduce-scatter.8
  970.8 44.5 reduce-scatter.22
  1017.9 72.4 reduce-scatter.20
  1093.2 134.0 reduce-scatter.18
  1230.1 134.2 reduce-scatter.12
  1367.1 134.1 reduce-scatter.14
  1504.0 140.6 reduce-scatter.16
  1647.4 140.5 reduce-scatter.10
where the time goes:
time: 1800 us
  waiting for transfers between devices  1150 us (64%)
  blocking collectives  340 us (19%)
  matrix products  128 us (7%)
  local copies, waits for them, and re-layouts  86.7 us (5%)
  other arithmetic  60.9 us (3%)
    all_gather x1, blocking collectives, local(): lax.all_gather(w_router, ('ctx', 'exp'), axis=0, tiled=True)  152 us
    reduce_scatter x1, waiting for transfers between devices, local(): lax.psum_scatter(grad_output_w, ('ctx', 'exp'), scatter_dimension=0, tile...  143 us
    reduce_scatter x1, waiting for transfers between devices, local(): lax.psum_scatter(grad_query_w, ('ctx', 'exp'), scatter_dimension=0, tiled...  143 us
    reduce_scatter x1, waiting for transfers between devices, local(): lax.psum_scatter(grad_key_w, ('ctx', 'exp'), scatter_dimension=0, tiled=T...  137 us
    reduce_scatter x1, waiting for transfers between devices, local(): lax.psum_scatter(grad_value_w, ('ctx', 'exp'), scatter_dimension=0, tiled...  137 us
    reduce_scatter x1, waiting for transfers between devices, local(): lax.psum_scatter(grad_router, ('ctx', 'exp'), scatter_dimension=0, tiled=...  133 us
    all_to_all x1, blocking collectives, local(): lax.all_to_all(grad_send, 'exp', split_axis=0, concat_axis=0, tiled=True)  105 us
    all_to_all x1, waiting for transfers between devices, local(): lax.all_to_all(send_rows, 'exp', split_axis=0, concat_axis=0, tiled=True)  104 us
  transfers between devices with their start and end apart: 19, of which 15 were waited for; matrix products, arithmetic and copies ran while one was open for 7% of the time, Pallas kernels for 0%

commit v1 on v0

--- a/solution.py
+++ b/solution.py
@@ -343,9 +343,281 @@
     return (mixed_out[None], grad_inputs[None]) + tuple(dense_sums) + tuple(expert_sums)
 
 
+def softmax_members(logits, member):
+    top = jnp.max(jnp.where(member, logits, MASK_FILLER), -1, keepdims=True)
+    weights = jnp.where(member, jnp.exp(logits - top), 0.0)
+    return weights / jnp.sum(weights, -1, keepdims=True)
+
+
+def two_parts(values):
+    high = values.astype(jnp.bfloat16)
+    return high, (values - high.astype(jnp.float32)).astype(jnp.bfloat16)
+
+
+def by_heads(
+    tokens,
+    segments,
+    routes,
+    gain_attn,
+    gain_moe,
+    query_weight,
+    key_weight,
+    value_weight,
+    w_output,
+    w_router,
+    w_expert_in,
+    w_expert_out,
+    cotangent,
+):
+    shards = lax.axis_size("ctx")
+    groups = lax.axis_size("exp")
+    exp_rank = lax.axis_index("exp")
+    local_experts = EXPERTS // groups
+    token_rows, width = tokens.shape[1], tokens.shape[2]
+    rows = query_weight.shape[0]
+    seq_len = token_rows * shards
+    q_cols = query_weight.shape[1] // shards
+    k_cols = key_weight.shape[1] // shards
+    kv_heads = KEY_VALUE_HEADS // shards
+    head_cluster = QUERY_HEADS // KEY_VALUE_HEADS
+    factor = 1.0 / math.sqrt(HEAD_SIZE)
+    main_cols = q_cols + 2 * k_cols
+    side = 128
+
+    expert_in = lax.all_gather(w_expert_in, "ctx", axis=1, tiled=True)
+    expert_out = lax.all_gather(w_expert_out, "ctx", axis=1, tiled=True)
+    all_tokens = lax.all_gather(tokens[0], "ctx", axis=0, tiled=True)
+    side_cols = jnp.concatenate(
+        [
+            w_router,
+            gain_attn[:, None],
+            gain_moe[:, None],
+            jnp.zeros((rows, side - EXPERTS - 2), jnp.bfloat16),
+        ],
+        1,
+    )
+    packed = jnp.concatenate(
+        [
+            query_weight.reshape(rows, shards, q_cols),
+            key_weight.reshape(rows, shards, k_cols),
+            value_weight.reshape(rows, shards, k_cols),
+            jnp.broadcast_to(side_cols[:, None, :], (rows, shards, side)),
+        ],
+        2,
+    ).transpose(1, 0, 2)
+    packed = lax.all_to_all(packed, "ctx", split_axis=0, concat_axis=0, tiled=True)
+    packed = lax.all_gather(packed, "exp", axis=1, tiled=True).reshape(width, main_cols + side)
+    w_main = packed[:, :main_cols]
+    router = packed[:, main_cols : main_cols + EXPERTS]
+    gain_one = packed[:, main_cols + EXPERTS].astype(jnp.float32)
+    gain_two = packed[:, main_cols + EXPERTS + 1].astype(jnp.float32)
+    out_rows = lax.all_gather(w_output, "exp", axis=0, tiled=True)
+    all_cot = lax.all_gather(cotangent[0], "exp", axis=0, tiled=False)
+    all_routes = lax.all_gather(routes[0], "exp", axis=0, tiled=False)
+
+    inputs_all = all_tokens.astype(jnp.float32)
+    scale_all = rms_scale(inputs_all)
+    normed = (inputs_all * scale_all * gain_one).astype(jnp.bfloat16)
+    qkv = jnp.dot(normed, w_main, preferred_element_type=jnp.float32).astype(jnp.bfloat16)
+    queries = qkv[:, :q_cols].reshape(seq_len, kv_heads, head_cluster, HEAD_SIZE)
+    keys = qkv[:, q_cols : q_cols + k_cols].reshape(seq_len, kv_heads, HEAD_SIZE)
+    values = qkv[:, q_cols + k_cols :].reshape(seq_len, kv_heads, HEAD_SIZE)
+    seg = segments[0]
+    pos = jnp.arange(seq_len, dtype=jnp.int32)
+    allowed = (pos[None, :] <= pos[:, None]) & (seg[None, :] == seg[:, None])
+    scores = (
+        jnp.einsum("ihgd,jhd->hgij", queries, keys, preferred_element_type=jnp.float32) * factor
+    )
+    scores = jnp.where(allowed, scores, MASK_FILLER)
+    top = jnp.max(scores, -1, keepdims=True)
+    weights = jnp.where(allowed, jnp.exp(scores - top), 0.0)
+    total = jnp.sum(weights, -1)
+    log_norm = top[..., 0] + jnp.log(total)
+    heads_out = jnp.einsum(
+        "hgij,jhd->ihgd", weights.astype(jnp.bfloat16), values, preferred_element_type=jnp.float32
+    ) / jnp.transpose(total, (2, 0, 1))[..., None]
+    attn_low = heads_out.reshape(seq_len, q_cols).astype(jnp.bfloat16)
+    branch_part = jnp.dot(attn_low, out_rows, preferred_element_type=jnp.float32).astype(jnp.bfloat16)
+    branch = lax.psum_scatter(branch_part, "ctx", scatter_dimension=0, tiled=True)
+    inputs = tokens[0].astype(jnp.float32)
+    resid = inputs + branch.astype(jnp.float32)
+    scale_two = rms_scale(resid)
+    moe_in = (resid * scale_two * gain_two).astype(jnp.bfloat16)
+
+    all_moe = lax.all_gather(moe_in, "exp", axis=0, tiled=False)
+    member = jnp.any(
+        all_routes[..., None] == jnp.arange(EXPERTS, dtype=jnp.int32), axis=2
+    )
+    logits = jnp.einsum("std,de->ste", all_moe, router, preferred_element_type=jnp.float32)
+    gates = softmax_members(logits, member)
+    earlier = jnp.tril(jnp.ones((token_rows, token_rows), jnp.bfloat16), -1)
+    rank = jnp.einsum(
+        "tu,sue->ste", earlier, member.astype(jnp.bfloat16), preferred_element_type=jnp.float32
+    ).astype(jnp.int32)
+    kept = member & (rank < CAP)
+    first = exp_rank * local_experts
+
+    def mine(table):
+        return lax.dynamic_slice_in_dim(table, first, local_experts, 2)
+
+    place = jnp.where(mine(kept), mine(rank), -1)
+    pick = (
+        place.transpose(0, 2, 1)[:, :, None, :]
+        == jnp.arange(CAP, dtype=jnp.int32)[None, None, :, None]
+    ).astype(jnp.bfloat16)
+    both = jnp.concatenate([all_moe, all_cot], -1)
+    slots = jnp.einsum("sjct,std->sjcd", pick, both, preferred_element_type=jnp.float32)
+    slot_rows = slots[..., :width].astype(jnp.bfloat16)
+    slot_cot = slots[..., width:]
+    slot_gate = jnp.sum(
+        pick.astype(jnp.float32) * mine(gates).transpose(0, 2, 1)[:, :, None, :], -1
+    )
+    pre = jnp.einsum("sjcd,jdf->sjcf", slot_rows, expert_in, preferred_element_type=jnp.float32)
+    gate_part, up_part = pre[..., :FF], pre[..., FF:]
+    sigmoid_gate = jax.nn.sigmoid(gate_part)
+    hidden = (gate_part * sigmoid_gate * up_part).astype(jnp.bfloat16)
+    expert_rows = jnp.einsum(
+        "sjcf,jfd->sjcd", hidden, expert_out, preferred_element_type=jnp.float32
+    ).astype(jnp.bfloat16)
+    weighted = (slot_gate[..., None] * expert_rows.astype(jnp.float32)).astype(jnp.bfloat16)
+    mixed_part = jnp.einsum(
+        "sjct,sjcd->std", pick, weighted, preferred_element_type=jnp.float32
+    ).astype(jnp.bfloat16)
+    mixed = lax.psum_scatter(mixed_part, "exp", scatter_dimension=0, tiled=False)
+    mixed_out = (resid + mixed.astype(jnp.float32)).astype(jnp.bfloat16)
+
+    grad_rows = (slot_gate[..., None] * slot_cot).astype(jnp.bfloat16)
+    slot_dot = jnp.sum(slot_cot * expert_rows.astype(jnp.float32), -1)
+    grad_picked = jnp.sum(pick.astype(jnp.float32) * slot_dot[..., None], 2).transpose(0, 2, 1)
+    grad_picked = lax.dynamic_update_slice_in_dim(jnp.zeros_like(gates), grad_picked, first, 2)
+    grad_logits = gates * (grad_picked - jnp.sum(gates * grad_picked, -1, keepdims=True))
+    logits_high, logits_low = two_parts(grad_logits)
+    grad_router = jnp.einsum(
+        "std,ste->de", all_moe, logits_high, preferred_element_type=jnp.float32
+    ) + jnp.einsum("std,ste->de", all_moe, logits_low, preferred_element_type=jnp.float32)
+    grad_hidden = jnp.einsum(
+        "sjcd,jfd->sjcf", grad_rows, expert_out, preferred_element_type=jnp.float32
+    )
+    grad_gate = grad_hidden * up_part * sigmoid_gate * (1.0 + gate_part * (1.0 - sigmoid_gate))
+    grad_up = grad_hidden * gate_part * sigmoid_gate
+    grad_pre = jnp.concatenate([grad_gate, grad_up], -1).astype(jnp.bfloat16)
+    grad_slots = jnp.einsum(
+        "sjcf,jdf->sjcd", grad_pre, expert_in, preferred_element_type=jnp.float32
+    ).astype(jnp.bfloat16)
+    moe_part = (
+        jnp.einsum("sjct,sjcd->std", pick, grad_slots, preferred_element_type=jnp.float32)
+        + jnp.einsum("ste,de->std", logits_high, router, preferred_element_type=jnp.float32)
+        + jnp.einsum("ste,de->std", logits_low, router, preferred_element_type=jnp.float32)
+    ).astype(jnp.bfloat16)
+    grad_moe_in = lax.psum_scatter(moe_part, "exp", scatter_dimension=0, tiled=False).astype(
+        jnp.float32
+    )
+    grad_expert_out = jnp.einsum(
+        "sjcf,sjcd->jfd", hidden, grad_rows, preferred_element_type=jnp.float32
+    ).astype(jnp.bfloat16)
+    grad_expert_in = jnp.einsum(
+        "sjcd,sjcf->jdf", slot_rows, grad_pre, preferred_element_type=jnp.float32
+    ).astype(jnp.bfloat16)
+
+    grad_out = cotangent[0].astype(jnp.float32)
+    weighted_two = grad_moe_in * gain_two
+    grad_gain_two = jnp.sum(grad_moe_in * resid * scale_two, 0)
+    cube_two = scale_two * scale_two * scale_two
+    grad_resid = (
+        grad_out
+        + scale_two * weighted_two
+        - resid * cube_two * jnp.mean(weighted_two * resid, -1, keepdims=True)
+    )
+    resid_low = lax.all_gather(grad_resid.astype(jnp.bfloat16), "ctx", axis=0, tiled=True)
+
+    grad_output_w = lax.psum_scatter(
+        inner_rows(attn_low, resid_low).astype(jnp.bfloat16), "exp", scatter_dimension=0, tiled=True
+    ).astype(jnp.float32)
+    grad_heads = (
+        outer_cols(resid_low, out_rows)
+        .astype(jnp.bfloat16)
+        .reshape(seq_len, kv_heads, head_cluster, HEAD_SIZE)
+    )
+    delta = jnp.transpose(jnp.sum(grad_heads.astype(jnp.float32) * heads_out, -1), (1, 2, 0))
+    probs = jnp.where(allowed, jnp.exp(scores - log_norm[..., None]), 0.0)
+    grad_probs = jnp.einsum(
+        "ihgd,jhd->hgij", grad_heads, values, preferred_element_type=jnp.float32
+    )
+    grad_scores = (probs * (grad_probs - delta[..., None])).astype(jnp.bfloat16)
+    grad_queries = jnp.einsum(
+        "hgij,jhd->ihgd", grad_scores, keys, preferred_element_type=jnp.float32
+    )
+    grad_keys = jnp.einsum(
+        "hgij,ihgd->jhd", grad_scores, queries, preferred_element_type=jnp.float32
+    )
+    grad_values = jnp.einsum(
+        "hgij,ihgd->jhd", probs.astype(jnp.bfloat16), grad_heads, preferred_element_type=jnp.float32
+    )
+    grad_qkv = jnp.concatenate(
+        [
+            (grad_queries * factor).reshape(seq_len, -1),
+            (grad_keys * factor).reshape(seq_len, -1),
+            grad_values.reshape(seq_len, -1),
+        ],
+        1,
+    ).astype(jnp.bfloat16)
+    normed_part = outer_cols(grad_qkv, w_main)
+    grad_gain_one = jnp.sum(normed_part * inputs_all * scale_all, 0)
+    grad_normed = lax.psum_scatter(
+        normed_part.astype(jnp.bfloat16), "ctx", scatter_dimension=0, tiled=True
+    ).astype(jnp.float32)
+    weighted_one = grad_normed * gain_one
+    scale_one = rms_scale(inputs)
+    cube_one = scale_one * scale_one * scale_one
+    grad_inputs = (
+        grad_resid
+        + scale_one * weighted_one
+        - inputs * cube_one * jnp.mean(weighted_one * inputs, -1, keepdims=True)
+    )
+
+    sums = jnp.concatenate(
+        [
+            inner_rows(normed, grad_qkv),
+            grad_router,
+            grad_gain_one[:, None],
+            grad_gain_two[:, None],
+            jnp.zeros((width, side - EXPERTS - 2), jnp.float32),
+        ],
+        1,
+    ).astype(jnp.bfloat16)
+    sums = sums.reshape(shards, groups, rows, main_cols + side).transpose(1, 0, 2, 3)
+    sums = lax.psum_scatter(sums, "exp", scatter_dimension=0, tiled=False)
+    sums = lax.all_to_all(sums, "ctx", split_axis=0, concat_axis=0, tiled=True).astype(jnp.float32)
+
+    def columns(low, count):
+        return sums[:, :, low : low + count].transpose(1, 0, 2).reshape(rows, -1)
+
+    side_sums = jnp.sum(sums[:, :, main_cols:], 0)
+    expert_in_sum = lax.psum_scatter(
+        grad_expert_in, "ctx", scatter_dimension=1, tiled=True
+    ).astype(jnp.float32)
+    expert_out_sum = lax.psum_scatter(
+        grad_expert_out, "ctx", scatter_dimension=1, tiled=True
+    ).astype(jnp.float32)
+    return (
+        mixed_out[None],
+        grad_inputs[None],
+        side_sums[:, EXPERTS],
+        side_sums[:, EXPERTS + 1],
+        columns(0, q_cols),
+        columns(q_cols, k_cols),
+        columns(q_cols + k_cols, k_cols),
+        grad_output_w,
+        side_sums[:, :EXPERTS],
+        expert_in_sum,
+        expert_out_sum,
+    )
+
+
 def solution(mesh):
+    whole_heads = KEY_VALUE_HEADS % mesh.shape["ctx"] == 0
     return jax.shard_map(
-        local,
+        by_heads if whole_heads else local,
         mesh=mesh,
         in_specs=(
             P("exp", "ctx", None),

time: 1800 us -> 969 us (0.54)
  waiting for transfers between devices: 1150 us -> 652 us
  blocking collectives: 340 us -> 73 us
  local copies, waits for them, and re-layouts: 86.7 us -> 27.9 us
  other arithmetic: 60.9 us -> 33.1 us
  matrix products: 128 us -> 154 us
    reduce_scatter x8 -> x7, waiting for transfers between devices: 761 us -> 370 us  [the longest x1 90.7 us: by_heads(): lax.psum_scatter(mixed_part, 'exp', scatter_dimension=0, tiled=False)]
    all_to_all x3 -> x1, waiting for transfers between devices: 207 us -> 0.01 us  [by_heads(): lax.all_to_all(sums, 'ctx', split_axis=0, concat_axis=0, tiled=True)]
    all_to_all x1, blocking collectives: 105 us -> 9.02 us  [by_heads(): lax.all_to_all(packed, 'ctx', split_axis=0, concat_axis=0, tiled=True)]
    all_gather x1 -> x2, blocking collectives: 152 us -> 63.9 us  [the longest x1 32.7 us: by_heads(): out_rows = lax.all_gather(w_output, 'exp', axis=0, tiled=True)]
    unnamed x2 -> x0, blocking collectives: 81.8 us -> none
    unnamed x16, waiting for transfers between devices: 3.58 us -> 72.2 us
    gather x5 -> x0, local copies, waits for them, and re-layouts: 56.5 us -> none  [the longest x1 14 us: local(): jnp.take(grad_back, safe_slot, axis=0)]
    all_gather x8 -> x7, waiting for transfers between devices: 178 us -> 210 us  [the longest x1 69.6 us: by_heads(): all_cot = lax.all_gather(cotangent[0], 'exp', axis=0, tiled=False)]
  transfers between devices with their start and end apart: 19 -> 16, of which waited for: 15 -> 14; matrix products, arithmetic and copies ran while one was open for 7% -> 13% of each run, Pallas kernels for 0% -> 0%
where the time goes in v1:
time: 969 us; the launch traced here: 959 us
  waiting for transfers between devices  652 us (67%)
  matrix products  154 us (16%)
  blocking collectives  73 us (8%)
  other arithmetic  33.1 us (3%)
  local copies, waits for them, and re-layouts  27.9 us (3%)
  between operations  15.1 us (2%)
    reduce_scatter x1, waiting for transfers between devices, by_heads(): lax.psum_scatter(mixed_part, 'exp', scatter_dimension=0, tiled=False)  90.7 us
    reduce_scatter x1, waiting for transfers between devices, by_heads(): lax.psum_scatter(moe_part, 'exp', scatter_dimension=0, tiled=False)  88.2 us
    unnamed x16, waiting for transfers between devices  72.2 us
    reduce_scatter x1, waiting for transfers between devices, by_heads(): lax.psum_scatter(grad_expert_in, 'ctx', scatter_dimension=1, tiled=True)  71.1 us
    all_gather x1, waiting for transfers between devices, by_heads(): all_cot = lax.all_gather(cotangent[0], 'exp', axis=0, tiled=False)  69.6 us
    reduce_scatter x1, waiting for transfers between devices, by_heads(): lax.psum_scatter(inner_rows(attn_low, resid_low).astype(jnp.bfloat16), 'e...  59.2 us
    all_gather x1, waiting for transfers between devices, by_heads(): expert_in = lax.all_gather(w_expert_in, 'ctx', axis=1, tiled=True)  45.7 us
    all_gather x1, waiting for transfers between devices, by_heads(): all_moe = lax.all_gather(moe_in, 'exp', axis=0, tiled=False)  40 us
  transfers between devices with their start and end apart: 16, of which 14 were waited for; matrix products, arithmetic and copies ran while one was open for 13% of the time, Pallas kernels for 0%

profile of v1, /device:TPU:0, one launch (start us, length us, event | category | flops | bytes accessed | tf_op | source)
XLA Modules:
  0.0 959.3 jit_solution(3122740152994366317)
XLA Ops:
  11.3 9.0 all_to_all.10
  21.9 32.7 %all_gather.32 = bf16[256,1024]{1,0:T(8,128)(2,1)S(1)} all-gather(bf16[32,1024]{1,0:T(8,128)(2,1)} %param.21), channel_id=1, replica_groups=mesh['ctx'=4,'exp'=8] {'exp'}, dimensions={0}, use_global_device_ids=true | all-gather | bytes 589824 | tf_op jit(solution)/shard_map/all_gather | solution.py:414
  55.9 8.6 all-gather.10.cloned.1.call-done
  64.6 3.5 copy.110
  69.5 18.1 %all-gather.20.cloned.1.call-done = bf16[1,1024,1024]{2,1,0:T(8,128)(2,1)} async-done(((bf16[1,256,1024]{2,1,0:T(8,128)(2,1)}), bf16[1,1024,1024]{2,1,0:T(8,128)(2,1)}) %all-gather.20.cloned.1.call-update) | async-done | bytes 2097168 | tf_op jit(solution)/shard_map/all_gather | solution.py:389
  89.7 3.2 convolution_convert_fusion.2
  93.1 3.1 fusion.8
  96.2 4.2 fusion.3
  101.9 5.9 fusion.137
  110.8 31.5 %reduce-scatter.11.cloned.1.call-done = bf16[256,1024]{1,0:T(8,128)(2,1)} async-done(((bf16[1024,1024]{1,0:T(8,128)(2,1)}), bf16[256,1024]{1,0:T(8,128)(2,1)}) %reduce-scatter.11.cloned.1.call-update) | async-done | bytes 524304 | tf_op jit(solution)/shard_map/reduce_scatter | solution.py:441
  147.6 31.2 %all_gather.33 = s32[8,256,8]{1,2,0:T(8,128)S(1)} all-gather(s32[1,256,8]{1,2,0:T(8,128)S(1)} %copy-done.32), channel_id=1, replica_groups=mesh['ctx'=4,'exp'=8] {'exp'}, dimensions={0}, use_global_device_ids=true | all-gather | bytes 73728 | tf_op jit(solution)/shard_map/all_gather | solution.py:416
  179.6 40.0 %all-gather.22.cloned.1.call-done = bf16[2048,1024]{1,0:T(8,128)(2,1)} async-done(((bf16[256,1024]{1,0:T(8,128)(2,1)}), bf16[2048,1024]{1,0:T(8,128)(2,1)}) %all-gather.22.cloned.1.call-update) | async-done | bytes 4194320 | tf_op jit(solution)/shard_map/all_gather | solution.py:447
  219.6 3.5 fusion.120
  223.9 69.6 %all-gather.12.cloned.1.call-done = bf16[8,256,1024]{2,1,0:T(8,128)(2,1)} async-done(((bf16[1,256,1024]{2,1,0:T(8,128)(2,1)}), bf16[8,256,1024]{2,1,0:T(8,128)(2,1)}) %all-gather.12.cloned.1.call-update) | async-done | bytes 4194320 | tf_op jit(solution)/shard_map/all_gather | solution.py:415
  293.5 12.3 %fusion.9 = f32[8,4,72,2048]{3,2,1,0:T(8,128)} fusion(bf16[8,256,1024]{2,1,0:T(8,128)(2,1)} %all-gather.12.cloned.1.call-done, bf16[8,256,1024]{2,1,0:T(8,128)(2,1)} %bitcast.295, s32[8,4,256]{2,1,0:T(4,128)S(1)} %fusion.121), kind=kOutput, calls=%fused_computation.19 | convolution fusion | flops 2433286144 | bytes 27295744 | tf_op jit(solution)/shard_map/sjct,std->sjcd/dot_general | solution.py:469
  305.8 45.7 %all-gather.14.cloned.1.call-done = bf16[4,1024,1024]{2,1,0:T(8,128)(2,1)} async-done(((bf16[4,256,1024]{2,1,0:T(8,128)(2,1)}), bf16[4,1024,1024]{2,1,0:T(8,128)(2,1)}) %all-gather.14.cloned.1.call-update) | async-done | bytes 8388624 | tf_op jit(solution)/shard_map/all_gather | solution.py:387
  351.6 10.1 %fusion.51 = f32[8,4,72,1024]{3,2,0,1:T(8,128)S(1)} fusion(bf16[4,1024,1024]{2,1,0:T(8,128)(2,1)} %all-gather.14.cloned.1.call-done, f32[8,4,72,2048]{3,2,1,0:T(8,128)} %fusion.9), kind=kOutput, calls=%fused_computation.70 | convolution fusion | flops 4831838208 | bytes 22544384 | tf_op jit(solution)/shard_map/sjcd,jdf->sjcf/dot_general | solution.py:475
  361.7 3.6 copy-done.6
  366.9 20.9 %all-gather.16.cloned.1.call-done = bf16[4,512,1024]{2,1,0:T(8,128)(2,1)} async-done(((bf16[4,128,1024]{2,1,0:T(8,128)(2,1)}), bf16[4,512,1024]{2,1,0:T(8,128)(2,1)}) %all-gather.16.cloned.1.call-update) | async-done | bytes 4194320 | tf_op jit(solution)/shard_map/all_gather | solution.py:388
  387.7 8.2 fusion.7
  397.6 9.5 fusion.30
  407.1 19.1 %fusion.16 = bf16[4,8,72,1024]{3,2,0,1:T(8,128)(2,1)S(1)} fusion(bf16[4,1024,1024]{2,1,0:T(8,128)(2,1)} %all-gather.14.cloned.1.call-done, bf16[8,4,72,512]{3,2,0,1:T(8,128)(2,1)} %get-tuple-element.21, bf16[8,4,72,512]{3,2,0,1:T(8,128)(2,1)} %get-tuple-element.20), kind=kOutput, calls=%fused_computation.29 | convolution fusion | flops 4841275392 | bytes 17825792 | tf_op jit(solution)/shard_map/sjcf,jdf->sjcd/dot_general | solution.py:504
  426.2 2.4 fusion.26
  431.0 4.2 fusion.15
  435.3 88.2 %reduce-scatter.15.cloned.1.call-done = bf16[1,256,1024]{2,1,0:T(8,128)(2,1)} async-done(((bf16[8,256,1024]{2,1,0:T(8,128)(2,1)}), bf16[1,256,1024]{2,1,0:T(8,128)(2,1)}) %reduce-scatter.15.cloned.1.call-update) | async-done | bytes 524304 | tf_op jit(solution)/shard_map/reduce_scatter | solution.py:512
  525.0 2.4 fusion.134
  527.5 9.2 bitcast_convert_fusion.1
  536.8 3.2 convolution_bitcast_fusion.1
  542.4 7.5 all-gather.18.cloned.1.call-done
  549.9 2.6 multiply_reduce_fusion
  552.6 9.8 %fusion.2 = bf16[2,2,1024,1024]{2,3,1,0:T(8,128)(2,1)S(1)} fusion(f32[2,1024,1024,2]{2,1,3,0:T(8,128)} %copy-done.4, f32[2,2,1024]{2,1,0:T(2,128)S(1)} %bitcast.342, f32[2,2,1024]{2,1,0:T(2,128)S(1)} %log_add_fusion, pred[1024,1024]{0,1:T(8,128)(4,1)S(1)} %copy-done.11, bf16[1024,2,64,1]{0,2,3,1:T(8,128)(2,1)S(1)} %bitcast.320, ...), kind=kOutput, calls=%fused_computation.4 | convolution fusion | flops 566231040 | bytes 27033600 | tf_op jit(solution)/shard_map/ihgd,jhd->hgij/dot_general | solution.py:543
  564.0 2.7 fusion.81
  566.7 9.3 fusion.78
  576.1 2.8 fusion.40
  580.1 3.7 convolution_convert_fusion.1
  583.9 4.0 concatenate.39
  588.0 3.1 convolution_convert_fusion.3
  591.9 7.0 bitcast_convert_fusion.2
  599.0 12.1 %bitcast_convert_fusion = bf16[4,1024,1024]{2,1,0:T(8,128)(2,1)} fusion(f32[8,4,72,2048]{3,2,1,0:T(8,128)} %fusion.9, bf16[8,4,72,512]{3,2,0,1:T(8,128)(2,1)} %get-tuple-element.21, bf16[8,4,72,512]{3,2,0,1:T(8,128)(2,1)S(1)} %copy-done.35), kind=kOutput, calls=%fused_computation.1 | convolution fusion | flops 4845469696 | bytes 17825792 | tf_op jit(solution)/shard_map/sjcd,sjcf->jdf/dot_general | solution.py:518
  612.3 2.8 convert_element_type.221
  615.1 68.9 %all-reduce.3.cloned.1.call-done = bf16[8,4,32,640]{3,2,0,1:T(8,128)(2,1)} async-done(((bf16[8,4,32,640]{3,2,0,1:T(8,128)(2,1)}), bf16[8,4,32,640]{3,2,0,1:T(8,128)(2,1)}) %all-reduce.3.cloned.1.call-update) | async-done | bytes 1310736
  686.3 3.3 all-to-all-start.1
  689.6 59.2 %reduce-scatter.19.cloned.1.call-done = bf16[32,1024]{1,0:T(8,128)(2,1)} async-done(((bf16[256,1024]{1,0:T(8,128)(2,1)}), bf16[32,1024]{1,0:T(8,128)(2,1)}) %reduce-scatter.19.cloned.1.call-update) | async-done | bytes 65552 | tf_op jit(solution)/shard_map/reduce_scatter | solution.py:533
  753.1 29.0 %reduce-scatter.17.cloned.1.call-done = bf16[256,1024]{1,0:T(8,128)(2,1)} async-done(((bf16[1024,1024]{1,0:T(8,128)(2,1)}), bf16[256,1024]{1,0:T(8,128)(2,1)}) %reduce-scatter.17.cloned.1.call-update) | async-done | bytes 524304 | tf_op jit(solution)/shard_map/reduce_scatter | solution.py:566
  783.4 90.7 %reduce-scatter.13.cloned.1.call-done = bf16[1,256,1024]{2,1,0:T(8,128)(2,1)} async-done(((bf16[8,256,1024]{2,1,0:T(8,128)(2,1)}), bf16[1,256,1024]{2,1,0:T(8,128)(2,1)}) %reduce-scatter.13.cloned.1.call-update) | async-done | bytes 524304 | tf_op jit(solution)/shard_map/reduce_scatter | solution.py:486
  874.1 3.0 fusion.101
  877.1 71.1 %reduce-scatter.21.cloned.1.call-done = bf16[4,256,1024]{2,1,0:T(8,128)(2,1)} async-done(((bf16[4,1024,1024]{2,1,0:T(8,128)(2,1)}), bf16[4,256,1024]{2,1,0:T(8,128)(2,1)}) %reduce-scatter.21.cloned.1.call-update) | async-done | bytes 2097168 | tf_op jit(solution)/shard_map/reduce_scatter | solution.py:596
  948.2 4.1 convert_element_type.219
  (161 shorter events, 44.3 us)
Async XLA Ops:
  7.2 2.4 copy-start
  7.2 57.4 %all-gather.10.cloned.1.call-start = ((), (), s32[]{:S(2)}) async-start(), calls=%async_computation.9 | async-start | bytes 1474560 | tf_op jit(solution)/shard_map/all_gather | solution.py:409
  21.1 66.6 %all-gather.20.cloned.1.call-start = ((), (), s32[]{:S(2)}) async-start(), calls=%async_computation.21 | async-start | bytes 2621440 | tf_op jit(solution)/shard_map/all_gather | solution.py:389
  21.8 120.5 %reduce-scatter.11.cloned.1.call-start = ((), (), s32[]{:S(2)}) async-start(), calls=%async_computation.10 | async-start | bytes 2621440 | tf_op jit(solution)/shard_map/reduce_scatter | solution.py:441
  54.6 53.3 %copy-start.16 = (bf16[256,1024]{1,0:T(8,128)(2,1)}, bf16[256,1024]{1,0:T(8,128)(2,1)S(1)}, u32[]{:S(2)}) copy-start(bf16[256,1024]{1,0:T(8,128)(2,1)S(1)} %all_gather.32) | copy-start | bytes 1572868
  55.9 44.4 %copy-start.10 = (pred[1024,1024]{0,1:T(8,128)(4,1)}, pred[1024,1024]{0,1:T(8,128)(4,1)S(1)}, u32[]{:S(2)}) copy-start(pred[1024,1024]{0,1:T(8,128)(4,1)S(1)} %fusion.45) | copy-start | bytes 3145732
  93.0 3.1 copy-start.23
  93.0 7.4 copy-start.29
  93.1 3.1 copy-start.12
  96.2 5.8 copy-start.4
  107.8 34.5 %copy-start.3 = (bf16[1,256,1024]{2,1,0:T(8,128)(2,1)S(1)}, bf16[1,256,1024]{2,1,0:T(8,128)(2,1)}, u32[]{:S(2)}) copy-start(bf16[1,256,1024]{2,1,0:T(8,128)(2,1)} %param.13) | copy-start | bytes 1572868
  110.7 36.9 %copy-start.32 = (s32[1,256,8]{1,2,0:T(8,128)S(1)}, s32[1,256,8]{1,2,0:T(8,128)}, u32[]{:S(2)}) copy-start(s32[1,256,8]{1,2,0:T(8,128)} %param.15) | copy-start | bytes 24580
  110.7 108.9 %all-gather.22.cloned.1.call-start = ((), (), s32[]{:S(2)}) async-start(), calls=%async_computation.22 | async-start | bytes 4718592 | tf_op jit(solution)/shard_map/all_gather | solution.py:447
  145.7 147.8 %all-gather.12.cloned.1.call-start = ((), (), s32[]{:S(2)}) async-start(), calls=%async_computation.11 | async-start | bytes 4718592 | tf_op jit(solution)/shard_map/all_gather | solution.py:415
  146.2 205.3 %all-gather.14.cloned.1.call-start = ((), (), s32[]{:S(2)}) async-start(), calls=%async_computation.12 | async-start | bytes 10485760 | tf_op jit(solution)/shard_map/all_gather | solution.py:387
  146.8 240.9 %all-gather.16.cloned.1.call-start = ((), (), s32[]{:S(2)}) async-start(), calls=%async_computation.13 | async-start | bytes 5242880 | tf_op jit(solution)/shard_map/all_gather | solution.py:388
  147.6 375.9 %reduce-scatter.15.cloned.1.call-start = ((), (), s32[]{:S(2)}) async-start(), calls=%async_computation.15 | async-start | bytes 4718592 | tf_op jit(solution)/shard_map/reduce_scatter | solution.py:512
  361.6 3.6 copy-start.6
  387.7 9.8 %copy-start.7 = (f32[8,4,72,1024]{3,2,0,1:T(8,128)S(1)}, f32[8,4,72,1024]{3,2,0,1:T(8,128)}, u32[]{:S(2)}) copy-start(f32[8,4,72,1024]{3,2,0,1:T(8,128)} %copy-done.6) | copy-start | bytes 28311556
  428.7 2.2 copy-start.20
  428.8 2.2 copy-start.22
  431.0 92.4 %copy-start.5 = (bf16[256,1024]{1,0:T(8,128)(2,1)S(1)}, bf16[256,1024]{1,0:T(8,128)(2,1)}, u32[]{:S(2)}) copy-start(bf16[256,1024]{1,0:T(8,128)(2,1)} %reduce-scatter.11.cloned.1.call-done) | copy-start | bytes 1572868
  435.2 114.7 %all-gather.18.cloned.1.call-start = ((), (), s32[]{:S(2)}) async-start(), calls=%async_computation.16 | async-start | bytes 2621440 | tf_op jit(solution)/shard_map/all_gather | solution.py:531
  527.4 84.9 %reduce-scatter.23.cloned.1.call-start = ((), (), s32[]{:S(2)}) async-start(), calls=%async_computation.20 | async-start | bytes 5242880 | tf_op jit(solution)/shard_map/reduce_scatter | solution.py:599
  536.6 3.4 copy-start.21
  536.7 147.4 %all-reduce.3.cloned.1.call-start = ((), (), s32[]{:S(2)}) async-start(), calls=%async_computation.23 | async-start | bytes 2621440
  536.7 3.5 copy-start.2
  536.7 13.2 %copy-start.17 = (bf16[256,1024]{1,0:T(8,128)(2,1)S(1)}, bf16[256,1024]{1,0:T(8,128)(2,1)}, u32[]{:S(2)}) copy-start(bf16[256,1024]{1,0:T(8,128)(2,1)} %copy-done.16) | copy-start | bytes 1572868
  541.1 11.5 %copy-start.11 = (pred[1024,1024]{0,1:T(8,128)(4,1)S(1)}, pred[1024,1024]{0,1:T(8,128)(4,1)}, u32[]{:S(2)}) copy-start(pred[1024,1024]{0,1:T(8,128)(4,1)} %copy-done.10) | copy-start | bytes 3145732
  541.1 11.5 %copy-start.30 = (bf16[1024,128]{0,1:T(8,128)(2,1)S(1)}, bf16[1024,128]{0,1:T(8,128)(2,1)}, u32[]{:S(2)}) copy-start(bf16[1024,128]{0,1:T(8,128)(2,1)} %copy-done.29) | copy-start | bytes 786436
  552.6 9.8 %copy-start.24 = (bf16[1024,128]{0,1:T(8,128)(2,1)S(1)}, bf16[1024,128]{0,1:T(8,128)(2,1)}, u32[]{:S(2)}) copy-start(bf16[1024,128]{0,1:T(8,128)(2,1)} %copy-done.23) | copy-start | bytes 786436
  564.0 12.1 %copy-start.25 = (bf16[2,64,2,1024]{3,1,2,0:T(8,128)(2,1)}, bf16[2,64,2,1024]{3,1,2,0:T(8,128)(2,1)S(1)}, u32[]{:S(2)}) copy-start(bf16[2,64,2,1024]{3,1,2,0:T(8,128)(2,1)S(1)} %fusion.71) | copy-start | bytes 1572868
  566.6 9.4 copy-start.28
  566.6 9.4 copy-start.14
  566.6 9.4 copy-start.19
  576.0 2.9 copy-start.33
  576.1 4.0 copy-start.15
  583.8 4.1 copy-start.27
  587.9 161.0 %reduce-scatter.19.cloned.1.call-start = ((), (), s32[]{:S(2)}) async-start(), calls=%async_computation.18 | async-start | bytes 589824 | tf_op jit(solution)/shard_map/reduce_scatter | solution.py:533
  591.1 191.0 %reduce-scatter.17.cloned.1.call-start = ((), (), s32[]{:S(2)}) async-start(), calls=%async_computation.17 | async-start | bytes 2621440 | tf_op jit(solution)/shard_map/reduce_scatter | solution.py:566
  591.8 282.2 %reduce-scatter.13.cloned.1.call-start = ((), (), s32[]{:S(2)}) async-start(), calls=%async_computation.14 | async-start | bytes 4718592 | tf_op jit(solution)/shard_map/reduce_scatter | solution.py:486
  591.9 7.1 copy-start.35
  598.9 349.3 %reduce-scatter.21.cloned.1.call-start = ((), (), s32[]{:S(2)}) async-start(), calls=%async_computation.19 | async-start | bytes 10485760 | tf_op jit(solution)/shard_map/reduce_scatter | solution.py:596
  611.1 263.0 %copy-start.8 = (bf16[1,256,1024]{2,1,0:T(8,128)(2,1)S(1)}, bf16[1,256,1024]{2,1,0:T(8,128)(2,1)}, u32[]{:S(2)}) copy-start(bf16[1,256,1024]{2,1,0:T(8,128)(2,1)} %param.25) | copy-start | bytes 1572868
  611.1 263.0 %copy-start.9 = (bf16[1,256,1024]{2,1,0:T(8,128)(2,1)S(1)}, bf16[1,256,1024]{2,1,0:T(8,128)(2,1)}, u32[]{:S(2)}) copy-start(bf16[1,256,1024]{2,1,0:T(8,128)(2,1)} %reduce-scatter.15.cloned.1.call-done) | copy-start | bytes 1572868
  686.3 64.1 %all-to-all-start.1 = ((bf16[4,32,640]{2,1,0:T(8,128)(2,1)}), bf16[4,32,640]{2,1,0:T(8,128)(2,1)S(1)}, u32[]{:S(2)}, u32[]{:S(2)}) async-start(bf16[4,32,640]{2,1,0:T(8,128)(2,1)} %dynamic-slice_bitcast_fusion), calls=%async_computation.5 | async-start | bytes 327680 | tf_op jit(solution)/shard_map/all_to_all | solution.py:590
  751.1 201.2 %copy-start.31 = (f32[32,128]{1,0:T(8,128)}, f32[32,128]{1,0:T(8,128)S(1)}, u32[]{:S(2)}) copy-start(f32[32,128]{1,0:T(8,128)S(1)} %get-tuple-element.32) | copy-start | bytes 49156
  874.1 78.2 %copy-start.1 = (bf16[32,512]{1,0:T(8,128)(2,1)S(1)}, bf16[32,512]{1,0:T(8,128)(2,1)}, u32[]{:S(2)}) copy-start(bf16[32,512]{1,0:T(8,128)(2,1)} %param.19) | copy-start | bytes 98308
  (4 other events, 4.1 us)
Sparse Core Ops, SparseCore 0:
  21.2 43.3 all-gather.9
  66.1 21.4 all-gather.19
  110.8 31.4 reduce-scatter.10
  145.8 73.7 all-gather.21
  221.8 71.6 all-gather.11
  295.0 56.5 all-gather.13
  353.2 34.4 all-gather.15
  435.3 88.0 reduce-scatter.14
  527.5 22.3 all-gather.17
  552.3 44.4 reduce-scatter.22
  600.8 83.1 all-reduce.2
  687.8 61.0 reduce-scatter.18
  751.6 30.4 reduce-scatter.16
  786.2 87.8 reduce-scatter.12
  876.7 71.4 reduce-scatter.20

commit v2 on v0

--- a/solution.py
+++ b/solution.py
@@ -3,6 +3,8 @@
 import jax
 import jax.numpy as jnp
 from jax import lax
+from jax.experimental import pallas as pl
+from jax.experimental.pallas import tpu as pltpu
 from jax.sharding import PartitionSpec as P
 
 QUERY_HEADS = 16
@@ -343,9 +345,1389 @@
     return (mixed_out[None], grad_inputs[None]) + tuple(dense_sums) + tuple(expert_sums)
 
 
+MESH = pl.DeviceIdType.MESH
+VMEM = pltpu.VMEM
+DMA = pltpu.SemaphoreType.DMA
+LINES = 4
+GRANT = 56 * 2**20
+
+
+def to_f32(value):
+    return value.astype(jnp.float32)
+
+
+def dot_rows(left, right):
+    return jnp.dot(left, right, preferred_element_type=jnp.float32)
+
+
+def remote(source, target, send, recv, to):
+    return pltpu.make_async_remote_copy(
+        src_ref=source,
+        dst_ref=target,
+        send_sem=send,
+        recv_sem=recv,
+        device_id=to,
+        device_id_type=MESH,
+    )
+
+
+class Place:
+    def __init__(self):
+        ctx, exp = lax.axis_index("ctx"), lax.axis_index("exp")
+        self.ctx, self.exp = ctx, exp
+        self.y, self.half = ctx // 2, ctx % 2
+        self.z, self.x = exp // 2, exp % 2
+        other_half = ctx + 1 - 2 * (ctx % 2)
+        self.up, self.down = (ctx, exp + 2), (ctx, exp - 2)
+        self.across = (ctx, exp + 1 - 2 * (exp % 2))
+        self.core = (other_half, exp)
+        self.side = (lax.rem(ctx + 2, 4), exp)
+        self.far = (lax.rem(other_half + 2, 4), exp)
+
+    def greet(self, lines=True, square=True):
+        barrier = pltpu.get_barrier_semaphore()
+        count = jnp.int32(0)
+        if square:
+            for to in (self.core, self.side, self.far):
+                pl.semaphore_signal(barrier, inc=1, device_id=to, device_id_type=MESH)
+            count = count + 3
+        if lines:
+            pl.semaphore_signal(barrier, inc=1, device_id=self.across, device_id_type=MESH)
+
+            @pl.when(self.z < LINES - 1)
+            def _():
+                pl.semaphore_signal(barrier, inc=1, device_id=self.up, device_id_type=MESH)
+
+            @pl.when(self.z > 0)
+            def _():
+                pl.semaphore_signal(barrier, inc=1, device_id=self.down, device_id_type=MESH)
+
+            count = count + 1 + jnp.where(self.z < LINES - 1, 1, 0) + jnp.where(self.z > 0, 1, 0)
+        pl.semaphore_wait(barrier, count)
+
+
+class ExpGather:
+    def __init__(self, place, view, parts, send, recv):
+        self.place, self.view, self.parts = place, view, parts
+        self.send, self.recv = send, recv
+
+    def copy(self, lane, line, part, to):
+        index = line * 2 + self.place.x
+        ref = self.view(index, part)
+        return remote(ref, ref, self.send.at[lane, line, part], self.recv.at[index, part], to)
+
+    def pass_on(self, line, part, up, down):
+        place = self.place
+        if up:
+
+            @pl.when(place.z < LINES - 1)
+            def _():
+                self.copy(1, line, part, place.up).start()
+
+        if down:
+
+            @pl.when(place.z > 0)
+            def _():
+                self.copy(2, line, part, place.down).start()
+
+        self.copy(0, line, part, place.across).start()
+
+    def begin(self, part):
+        self.pass_on(self.place.z, part, True, True)
+
+    def arrived(self, index, part):
+        ref = self.view(index, part)
+        remote(
+            ref, ref, self.send.at[0, 0, part], self.recv.at[index, part], self.place.across
+        ).wait_recv()
+
+    def relay(self, step, part):
+        place = self.place
+
+        @pl.when(place.z >= step)
+        def _():
+            line = place.z - step
+            self.arrived(line * 2 + place.x, part)
+            self.pass_on(line, part, True, False)
+
+        @pl.when(place.z + step < LINES)
+        def _():
+            line = place.z + step
+            self.arrived(line * 2 + place.x, part)
+            self.pass_on(line, part, False, True)
+
+    def relays(self):
+        for step in range(1, LINES):
+            for part in range(self.parts):
+                self.relay(step, part)
+
+    def across_arrived(self, line, part):
+        self.arrived(line * 2 + 1 - self.place.x, part)
+
+    def finish(self):
+        place = self.place
+        for part in range(self.parts):
+            for line in range(LINES):
+                self.across_arrived(line, part)
+        for part in range(self.parts):
+            for line in range(LINES):
+                self.copy(0, line, part, place.across).wait_send()
+
+                @pl.when((place.z >= line) & (place.z < LINES - 1))
+                def _():
+                    self.copy(1, line, part, place.up).wait_send()
+
+                @pl.when((place.z <= line) & (place.z > 0))
+                def _():
+                    self.copy(2, line, part, place.down).wait_send()
+
+
+def gather_sems(parts):
+    return [DMA((3, LINES, parts)), DMA((2 * LINES, parts))]
+
+
+def raised_slot(line):
+    return max(line - 1, 0) if isinstance(line, int) else jnp.maximum(line - 1, 0)
+
+
+def lowered_slot(line):
+    return min(line, LINES - 2) if isinstance(line, int) else jnp.minimum(line, LINES - 2)
+
+
+class ExpScatter:
+    def __init__(self, place, outgoing, mine, crossed, raised, lowered, parts, sems):
+        self.place, self.parts = place, parts
+        self.outgoing, self.mine = outgoing, mine
+        self.crossed, self.raised, self.lowered = crossed, raised, lowered
+        self.cross_send, self.cross_recv, self.line_send, self.line_recv = sems
+
+    def cross(self, line, part):
+        place = self.place
+        return remote(
+            self.outgoing(line, part),
+            self.crossed(line, part),
+            self.cross_send.at[line, part],
+            self.cross_recv.at[line, part],
+            place.across,
+        )
+
+    def along(self, up, line, part):
+        place = self.place
+        side = 0 if up else 1
+        return remote(
+            self.mine(line, part),
+            (self.raised if up else self.lowered)(line, part),
+            self.line_send.at[side, line, part],
+            self.line_recv.at[side, line, part],
+            place.up if up else place.down,
+        )
+
+    def begin(self, line, part):
+        self.cross(line, part).start()
+
+    def fold(self, line, part):
+        place = self.place
+
+        @pl.when(place.z != line)
+        def _():
+            self.cross(line, part).wait_recv()
+            ref = self.mine(line, part)
+            ref[...] = (to_f32(ref[...]) + to_f32(self.crossed(line, part)[...])).astype(ref.dtype)
+
+        for up in (True, False):
+            towards = place.z < line if up else place.z > line
+            inner = place.z > 0 if up else place.z < LINES - 1
+
+            @pl.when(towards)
+            def _():
+                ref = self.mine(line, part)
+
+                @pl.when(inner)
+                def _():
+                    self.along(up, line, part).wait_recv()
+                    came = (self.raised if up else self.lowered)(line, part)
+                    ref[...] = (to_f32(ref[...]) + to_f32(came[...])).astype(ref.dtype)
+
+                self.along(up, line, part).start()
+
+    def total(self, part):
+        place = self.place
+        line = place.z
+        self.cross(line, part).wait_recv()
+        value = to_f32(self.mine(line, part)[...]) + to_f32(self.crossed(line, part)[...])
+        for up in (True, False):
+            came = (self.raised if up else self.lowered)(line, part)
+            some = line > 0 if up else line < LINES - 1
+
+            @pl.when(some)
+            def _():
+                self.along(up, line, part).wait_recv()
+
+            value = value + jnp.where(some, to_f32(came[...]), 0.0)
+        return value
+
+    def finish(self):
+        place = self.place
+        for part in range(self.parts):
+            for line in range(LINES):
+                self.cross(line, part).wait_send()
+                for up in (True, False):
+
+                    @pl.when(place.z < line if up else place.z > line)
+                    def _():
+                        self.along(up, line, part).wait_send()
+
+
+def scatter_sems(parts):
+    return [DMA((LINES, parts)), DMA((LINES, parts)), DMA((2, LINES, parts)), DMA((2, LINES, parts))]
+
+
+class CtxGather:
+    def __init__(self, place, view, parts, send, recv):
+        self.place, self.view, self.parts = place, view, parts
+        self.send, self.recv = send, recv
+
+    def copy(self, lane, part):
+        place = self.place
+        index = lax.rem(place.ctx + 2, 4) if lane == 2 else place.ctx
+        ref = self.view(index, part)
+        to = place.side if lane == 1 else place.core
+        return remote(ref, ref, self.send.at[lane, part], self.recv.at[lane, part], to)
+
+    def landed(self, lane, part):
+        place = self.place
+        index = (place.core, place.side, place.far)[lane][0]
+        ref = self.view(index, part)
+        return remote(ref, ref, self.send.at[lane, part], self.recv.at[lane, part], place.core)
+
+    def begin(self, part):
+        self.copy(1, part).start()
+        self.copy(0, part).start()
+
+    def relay(self, part):
+        self.landed(1, part).wait_recv()
+        self.copy(2, part).start()
+
+    def arrived(self, part):
+        self.landed(0, part).wait_recv()
+        self.landed(2, part).wait_recv()
+
+    def sent(self, part):
+        for lane in range(3):
+            self.copy(lane, part).wait_send()
+
+
+def square_sems(parts):
+    return [DMA((3, parts)), DMA((3, parts))]
+
+
+class CtxScatter:
+    def __init__(self, place, outgoing, mine, swapped, crossed, parts, send, recv):
+        self.place, self.parts = place, parts
+        self.outgoing, self.mine = outgoing, mine
+        self.swapped, self.crossed = swapped, crossed
+        self.send, self.recv = send, recv
+
+    def swap(self, near, part):
+        place = self.place
+        y = place.y if near else 1 - place.y
+        lane = 0 if near else 1
+        return remote(
+            self.outgoing(y, part),
+            self.swapped(lane, part),
+            self.send.at[lane, part],
+            self.recv.at[lane, part],
+            place.core,
+        )
+
+    def over(self, part):
+        place = self.place
+        return remote(
+            self.mine(1 - place.y, part),
+            self.crossed(part),
+            self.send.at[2, part],
+            self.recv.at[2, part],
+            place.side,
+        )
+
+    def fold(self, part):
+        self.swap(False, part).wait_recv()
+        ref = self.mine(1 - self.place.y, part)
+        ref[...] = (to_f32(ref[...]) + to_f32(self.swapped(1, part)[...])).astype(ref.dtype)
+        self.over(part).start()
+
+    def total(self, part):
+        self.swap(True, part).wait_recv()
+        self.over(part).wait_recv()
+        return (
+            to_f32(self.mine(self.place.y, part)[...])
+            + to_f32(self.swapped(0, part)[...])
+            + to_f32(self.crossed(part)[...])
+        )
+
+    def finish(self):
+        for part in range(self.parts):
+            self.swap(False, part).wait_send()
+            self.swap(True, part).wait_send()
+            self.over(part).wait_send()
+
+
+def front_kernel(
+    tokens,
+    side_cols,
+    wq,
+    wk,
+    wv,
+    wo,
+    routes,
+    seg_col,
+    seg_row,
+    cot,
+    exp_in,
+    exp_out,
+    all_moe,
+    all_cot,
+    all_routes,
+    all_in,
+    all_out,
+    all_tokens,
+    weights,
+    out_rows,
+    qkv,
+    heads_out,
+    log_norm,
+    resid_out,
+    packed,
+    partial,
+    swapped,
+    crossed,
+    stage,
+    local_sem,
+    tok_send,
+    tok_recv,
+    mix_send,
+    mix_recv,
+    w_send,
+    w_recv,
+    o_send,
+    o_recv,
+    r_send,
+    r_recv,
+    c_send,
+    c_recv,
+    m_send,
+    m_recv,
+    i_send,
+    i_recv,
+    u_send,
+    u_recv,
+    s_send,
+    s_recv,
+):
+    place = Place()
+    ctx, exp = place.ctx, place.exp
+    shards, rows = packed.shape[0], packed.shape[1]
+    token_rows, width = tokens.shape
+    q_cols = wq.shape[1] // shards
+    k_cols = wk.shape[1] // shards
+    main_cols = q_cols + 2 * k_cols
+    factor = 1.0 / math.sqrt(HEAD_SIZE)
+    keep = [
+        pltpu.make_async_copy(cot, all_cot.at[exp], local_sem.at[0]),
+        pltpu.make_async_copy(exp_in, all_in.at[:, ctx], local_sem.at[1]),
+        pltpu.make_async_copy(exp_out, all_out.at[:, ctx], local_sem.at[2]),
+    ]
+    for copy in keep:
+        copy.start()
+    all_tokens[ctx] = tokens[...]
+    for shard in range(shards):
+        packed[shard, :, :q_cols] = wq[:, shard * q_cols : (shard + 1) * q_cols]
+        packed[shard, :, q_cols : q_cols + k_cols] = wk[:, shard * k_cols : (shard + 1) * k_cols]
+        packed[shard, :, q_cols + k_cols : main_cols] = wv[:, shard * k_cols : (shard + 1) * k_cols]
+        packed[shard, :, main_cols:] = side_cols[...]
+    weights[ctx, exp] = packed[ctx]
+    out_rows[exp] = wo[...]
+    all_routes[exp] = routes[...]
+    place.greet()
+
+    mixes = []
+    for lane, to in enumerate((place.core, place.side, place.far)):
+        copy = remote(
+            packed.at[to[0]],
+            weights.at[ctx, exp],
+            mix_send.at[lane],
+            mix_recv.at[lane],
+            to,
+        )
+        copy.start()
+        mixes.append(copy)
+    token_gather = CtxGather(
+        place,
+        lambda index, part: all_tokens.at[index, pl.ds(part * (token_rows // 2), token_rows // 2)],
+        2,
+        tok_send,
+        tok_recv,
+    )
+    for part in range(2):
+        token_gather.begin(part)
+    route_gather = ExpGather(place, lambda index, part: all_routes.at[index], 1, r_send, r_recv)
+    weight_gather = ExpGather(place, lambda index, part: weights.at[:, index], 1, w_send, w_recv)
+    out_gather = ExpGather(place, lambda index, part: out_rows.at[index], 1, o_send, o_recv)
+    for lane, copy in enumerate(mixes):
+        source = (place.core, place.side, place.far)[lane][0]
+        remote(
+            packed.at[0], weights.at[source, exp], mix_send.at[lane], mix_recv.at[lane], place.core
+        ).wait_recv()
+    weight_gather.begin(0)
+    route_gather.begin(0)
+    out_gather.begin(0)
+    for part in range(2):
+        token_gather.relay(part)
+    for step in range(1, LINES):
+        weight_gather.relay(step, 0)
+        route_gather.relay(step, 0)
+        out_gather.relay(step, 0)
+
+    for copy in keep:
+        copy.wait()
+    local_experts = exp_in.shape[0]
+    in_gather = CtxGather(
+        place, lambda index, part: all_in.at[part, index], local_experts, i_send, i_recv
+    )
+    down_gather = CtxGather(
+        place, lambda index, part: all_out.at[part, index], local_experts, u_send, u_recv
+    )
+    cot_parts = 2
+    cot_rows = token_rows // cot_parts
+    cot_gather = ExpGather(
+        place,
+        lambda index, part: all_cot.at[index, pl.ds(part * cot_rows, cot_rows)],
+        cot_parts,
+        c_send,
+        c_recv,
+    )
+    for part in range(2):
+        token_gather.arrived(part)
+    weight_gather.finish()
+    for part in range(cot_parts):
+        cot_gather.begin(part)
+    for part in range(local_experts):
+        in_gather.begin(part)
+
+    gain_pick = (
+        lax.broadcasted_iota(jnp.int32, (8, weights.shape[3] - main_cols), 1)
+        == EXPERTS + lax.broadcasted_iota(jnp.int32, (8, weights.shape[3] - main_cols), 0)
+    ).astype(jnp.bfloat16)
+    full = weights[...].reshape(width, weights.shape[3])
+    gains = outer_cols(gain_pick, full[:, main_cols:])
+    gain_one, gain_two = gains[0:1], gains[1:2]
+    for block in range(shards):
+        values = to_f32(all_tokens[block])
+        normed = (values * rms_scale(values) * gain_one).astype(jnp.bfloat16)
+        qkv[pl.ds(block * token_rows, token_rows), :] = dot_rows(normed, full[:, :main_cols]).astype(
+            jnp.bfloat16
+        )
+    out_gather.finish()
+    route_gather.finish()
+
+    low = lax.broadcasted_iota(jnp.int32, (1, 2 * HEAD_SIZE), 1) < HEAD_SIZE
+
+    def spread(first):
+        plain = to_f32(qkv[:, first : first + k_cols])
+        turned = pltpu.roll(plain, HEAD_SIZE, 1)
+        zero = jnp.zeros((), jnp.float32)
+        return [
+            [
+                jnp.where(low, plain, zero).astype(jnp.bfloat16),
+                jnp.where(low, zero, turned).astype(jnp.bfloat16),
+            ],
+            [
+                jnp.where(low, turned, zero).astype(jnp.bfloat16),
+                jnp.where(low, zero, plain).astype(jnp.bfloat16),
+            ],
+        ]
+
+    keys, values = spread(q_cols), spread(q_cols + k_cols)
+    full_out = out_rows[...].reshape(q_cols, width)
+    for block in range(shards - 1, -1, -1):
+        here = pl.ds(block * token_rows, token_rows)
+        count = (block + 1) * token_rows
+        at_row = block * token_rows + lax.broadcasted_iota(jnp.int32, (token_rows, 1), 0)
+        at_col = lax.broadcasted_iota(jnp.int32, (1, count), 1)
+        bias = jnp.where(
+            (at_col <= at_row) & (seg_col[here, :] == seg_row[:, :count]), 0.0, MASK_FILLER
+        )
+        lows = []
+        norms = jnp.zeros((token_rows, 128), jnp.float32)
+        at_lane = lax.broadcasted_iota(jnp.int32, (1, 128), 1)
+        for pair in range(2):
+            queries = qkv[here, pair * 128 : pair * 128 + 128]
+            heads = jnp.zeros((token_rows, 128), jnp.float32)
+            for head in range(2):
+                scores = outer_cols(queries, keys[pair][head][:count]) * factor + bias
+                top = jnp.max(scores, -1, keepdims=True)
+                shares = jnp.exp(scores - top)
+                total = jnp.sum(shares, -1, keepdims=True)
+                norms = jnp.where(at_lane == 2 * pair + head, top + jnp.log(total), norms)
+                heads = heads + dot_rows(
+                    shares.astype(jnp.bfloat16), values[pair][head][:count]
+                ) / total
+            heads_out[here, pair * 128 : pair * 128 + 128] = heads
+            lows.append(heads.astype(jnp.bfloat16))
+        log_norm[here, :] = norms
+        partial[block] = dot_rows(jnp.concatenate(lows, 1), full_out).astype(jnp.bfloat16)
+        if block == 3:
+            for part in range(cot_parts):
+                cot_gather.relay(1, part)
+        if block == 2:
+            for part in range(local_experts // 2):
+                in_gather.relay(part)
+        if block == 1:
+            for part in range(cot_parts):
+                cot_gather.relay(2, part)
+
+    half_rows = token_rows // 2
+    branch = CtxScatter(
+        place,
+        lambda y, part: partial.at[2 * y + 1 - place.half, pl.ds(part * half_rows, half_rows)],
+        lambda y, part: partial.at[2 * y + place.half, pl.ds(part * half_rows, half_rows)],
+        lambda lane, part: swapped.at[lane, pl.ds(part * half_rows, half_rows)],
+        lambda part: crossed.at[pl.ds(part * half_rows, half_rows)],
+        2,
+        s_send,
+        s_recv,
+    )
+    for part in range(2):
+        branch.swap(False, part).start()
+    for part in range(2):
+        branch.swap(True, part).start()
+    for part in range(2):
+        branch.fold(part)
+    moe_parts = 4
+    moe_rows = token_rows // moe_parts
+    moe_gather = ExpGather(
+        place,
+        lambda index, part: all_moe.at[index, pl.ds(part * moe_rows, moe_rows)],
+        moe_parts,
+        m_send,
+        m_recv,
+    )
+    for part in range(2):
+        here = pl.ds(part * half_rows, half_rows)
+        resid = to_f32(tokens[here, :]) + branch.total(part)
+        resid_out[here, :] = resid
+        stage[here, :] = (resid * rms_scale(resid) * gain_two).astype(jnp.bfloat16)
+        copy = pltpu.make_async_copy(
+            stage.at[here], all_moe.at[exp, here], local_sem.at[3 + part]
+        )
+        copy.start()
+        copy.wait()
+        for piece in range(2):
+            moe_gather.begin(2 * part + piece)
+    for part in range(local_experts):
+        down_gather.begin(part)
+    for part in range(cot_parts):
+        cot_gather.relay(3, part)
+    for part in range(local_experts // 2, local_experts):
+        in_gather.relay(part)
+    moe_gather.relays()
+    for part in range(local_experts):
+        down_gather.relay(part)
+    moe_gather.finish()
+    cot_gather.finish()
+    branch.finish()
+    for part in range(2):
+        token_gather.sent(part)
+    for copy in mixes:
+        copy.wait_send()
+    for part in range(local_experts):
+        in_gather.arrived(part)
+        in_gather.sent(part)
+        down_gather.arrived(part)
+        down_gather.sent(part)
+
+
+def front(tokens, side_cols, wq, wk, wv, wo, routes, seg_col, seg_row, cot, exp_in, exp_out):
+    shards, groups = lax.axis_size("ctx"), lax.axis_size("exp")
+    token_rows, width = tokens.shape
+    rows = wq.shape[0]
+    q_cols, k_cols = wq.shape[1] // shards, wk.shape[1] // shards
+    pack_cols = q_cols + 2 * k_cols + side_cols.shape[1]
+    seq_len = token_rows * shards
+    low, f32 = jnp.bfloat16, jnp.float32
+    experts, in_rows, in_cols = exp_in.shape
+    out_count = exp_out.shape[1]
+
+    def shape(dims, dtype):
+        return jax.ShapeDtypeStruct(dims, dtype)
+
+    whole, anywhere = pl.BlockSpec(memory_space=VMEM), pl.BlockSpec(memory_space=pl.ANY)
+    return pl.pallas_call(
+        front_kernel,
+        name="front",
+        out_shape=[
+            shape((groups, token_rows, width), low),
+            shape((groups, token_rows, width), low),
+            shape((groups,) + routes.shape, jnp.int32),
+            shape((experts, shards, in_rows, in_cols), low),
+            shape((experts, shards, out_count, width), low),
+            shape((shards, token_rows, width), low),
+            shape((shards, groups, rows, pack_cols), low),
+            shape((groups, rows, width), low),
+            shape((seq_len, q_cols + 2 * k_cols), low),
+            shape((seq_len, q_cols), f32),
+            shape((seq_len, 128), f32),
+            shape((token_rows, width), f32),
+        ],
+        in_specs=[whole] * 9 + [anywhere] * 3,
+        out_specs=[anywhere] * 2 + [whole] + [anywhere] * 2 + [whole] * 7,
+        scratch_shapes=[
+            VMEM((shards, rows, pack_cols), low),
+            VMEM((shards, token_rows, width), low),
+            VMEM((2, token_rows, width), low),
+            VMEM((token_rows, width), low),
+            VMEM((token_rows, width), low),
+            DMA((5,)),
+            *square_sems(2),
+            DMA((3,)),
+            DMA((3,)),
+            *gather_sems(1),
+            *gather_sems(1),
+            *gather_sems(1),
+            *gather_sems(2),
+            *gather_sems(4),
+            *square_sems(experts),
+            *square_sems(experts),
+            *square_sems(2),
+        ],
+        compiler_params=pltpu.CompilerParams(
+            collective_id=0, has_side_effects=True, vmem_limit_bytes=GRANT
+        ),
+    )(tokens, side_cols, wq, wk, wv, wo, routes, seg_col, seg_row, cot, exp_in, exp_out)
+
+
+def back_kernel(
+    moe_part,
+    mixed_part,
+    grad_in,
+    grad_down,
+    tokens,
+    cot,
+    resid,
+    gain_two,
+    gain_one,
+    router_sum,
+    all_tokens,
+    weights,
+    out_rows,
+    qkv,
+    heads_out,
+    log_norm,
+    seg_col,
+    seg_row,
+    mixed_out,
+    grad_tokens,
+    query_sum,
+    key_sum,
+    value_sum,
+    side_sum,
+    output_sum,
+    in_sum,
+    down_sum,
+    moe_mine,
+    moe_crossed,
+    moe_raised,
+    moe_lowered,
+    mix_mine,
+    mix_crossed,
+    mix_raised,
+    mix_lowered,
+    in_mine,
+    in_swapped,
+    in_crossed,
+    down_mine,
+    down_swapped,
+    down_crossed,
+    grad_resid,
+    all_resid,
+    head_grads,
+    turned,
+    key_grads,
+    value_grads,
+    qkv_grads,
+    sums,
+    sums_crossed,
+    sums_raised,
+    sums_lowered,
+    sums_own,
+    sums_all,
+    out_grads,
+    out_crossed,
+    out_raised,
+    out_lowered,
+    in_stage,
+    down_stage,
+    store_sem,
+    local_sem,
+    token_sem,
+    moe_xs,
+    moe_xr,
+    moe_ls,
+    moe_lr,
+    mix_xs,
+    mix_xr,
+    mix_ls,
+    mix_lr,
+    sum_xs,
+    sum_xr,
+    sum_ls,
+    sum_lr,
+    out_xs,
+    out_xr,
+    out_ls,
+    out_lr,
+    in_send,
+    in_recv,
+    down_send,
+    down_recv,
+    normed_send,
+    normed_recv,
+    resid_send,
+    resid_recv,
+    last_send,
+    last_recv,
+):
+    place = Place()
+    ctx, exp = place.ctx, place.exp
+    token_rows, width = tokens.shape
+    shards, groups, rows, pack_cols = weights.shape
+    local_experts = grad_in.shape[0]
+    q_cols = heads_out.shape[1]
+    main_cols = qkv.shape[1]
+    k_cols = (main_cols - q_cols) // 2
+    factor = 1.0 / math.sqrt(HEAD_SIZE)
+    order = (3, 0, 2, 1)
+
+    loads = []
+
+    def load(source, target):
+        copy = pltpu.make_async_copy(source, target, local_sem.at[len(loads)])
+        copy.start()
+        loads.append(copy)
+
+    for line in order:
+        load(moe_part.at[line * 2 + place.x], moe_mine.at[line])
+    for y in range(2):
+        load(grad_in.at[:, 2 * y + place.half], in_mine.at[y])
+        load(grad_down.at[:, 2 * y + place.half], down_mine.at[y])
+    for line in order:
+        load(mixed_part.at[line * 2 + place.x], mix_mine.at[line])
+    place.greet()
+
+    def piece(ref, count, part):
+        size = ref.shape[0] // count
+        return ref.at[pl.ds(part * size, size)]
+
+    moe_parts, mix_parts = 4, 2
+    moe = ExpScatter(
+        place,
+        lambda line, part: piece(moe_part.at[line * 2 + 1 - place.x], moe_parts, part),
+        lambda line, part: piece(moe_mine.at[line], moe_parts, part),
+        lambda line, part: piece(moe_crossed.at[line], moe_parts, part),
+        lambda line, part: piece(moe_raised.at[raised_slot(line)], moe_parts, part),
+        lambda line, part: piece(moe_lowered.at[lowered_slot(line)], moe_parts, part),
+        moe_parts,
+        (moe_xs, moe_xr, moe_ls, moe_lr),
+    )
+    mix = ExpScatter(
+        place,
+        lambda line, part: piece(mixed_part.at[line * 2 + 1 - place.x], mix_parts, part),
+        lambda line, part: piece(mix_mine.at[line], mix_parts, part),
+        lambda line, part: piece(mix_crossed.at[line], mix_parts, part),
+        lambda line, part: piece(mix_raised.at[raised_slot(line)], mix_parts, part),
+        lambda line, part: piece(mix_lowered.at[lowered_slot(line)], mix_parts, part),
+        mix_parts,
+        (mix_xs, mix_xr, mix_ls, mix_lr),
+    )
+    into = CtxScatter(
+        place,
+        lambda y, part: grad_in.at[part, 2 * y + 1 - place.half],
+        lambda y, part: in_mine.at[y, part],
+        lambda lane, part: in_swapped.at[lane, part],
+        lambda part: in_crossed.at[part],
+        local_experts,
+        in_send,
+        in_recv,
+    )
+    downs = CtxScatter(
+        place,
+        lambda y, part: grad_down.at[part, 2 * y + 1 - place.half],
+        lambda y, part: down_mine.at[y, part],
+        lambda lane, part: down_swapped.at[lane, part],
+        lambda part: down_crossed.at[part],
+        local_experts,
+        down_send,
+        down_recv,
+    )
+    for first, second in ((3, 0), (2, 1)):
+        for part in range(moe_parts):
+            moe.begin(first, part)
+            moe.begin(second, part)
+    for near in (False, True):
+        for part in range(local_experts):
+            into.swap(near, part).start()
+        for part in range(local_experts):
+            downs.swap(near, part).start()
+    for copy in loads:
+        copy.wait()
+
+    expert = 0
+    for first, second in ((3, 0), (2, 1)):
+        for part in range(moe_parts):
+            moe.fold(first, part)
+            moe.fold(second, part)
+            if part % 2 == 1:
+                into.fold(expert)
+                expert += 1
+    gain_one_row, gain_two_row = gain_one[...], gain_two[...]
+    moe_rows = token_rows // moe_parts
+    gain_two_sum = jnp.zeros((1, width), jnp.float32)
+    resid_gather = CtxGather(
+        place,
+        lambda index, part: all_resid.at[index, pl.ds(part * moe_rows, moe_rows)],
+        moe_parts,
+        resid_send,
+        resid_recv,
+    )
+    for part in range(moe_parts):
+        here = pl.ds(part * moe_rows, moe_rows)
+        grad_moe_in = moe.total(part)
+        values = resid[here, :]
+        scale = rms_scale(values)
+        weighted = grad_moe_in * gain_two_row
+        gain_two_sum = gain_two_sum + jnp.sum(grad_moe_in * values * scale, 0, keepdims=True)
+        grads = (
+            to_f32(cot[here, :])
+            + scale * weighted
+            - values * (scale * scale * scale) * jnp.mean(weighted * values, -1, keepdims=True)
+        )
+        grad_resid[here, :] = grads
+        all_resid[ctx, here, :] = grads.astype(jnp.bfloat16)
+        resid_gather.begin(part)
+    for first, second in ((3, 0), (2, 1)):
+        for part in range(mix_parts):
+            mix.begin(first, part)
+            mix.begin(second, part)
+    moe.finish()
+    token_blocks, normed_part = moe_crossed, moe_mine
+    token_load = pltpu.make_async_copy(all_tokens, token_blocks, token_sem)
+    token_load.start()
+
+    full = weights[...].reshape(width, pack_cols)
+    full_out = out_rows[...].reshape(q_cols, width)
+    low = lax.broadcasted_iota(jnp.int32, (1, 2 * HEAD_SIZE), 1) < HEAD_SIZE
+
+    def spread(first):
+        plain = to_f32(qkv[:, first : first + k_cols])
+        other = pltpu.roll(plain, HEAD_SIZE, 1)
+        zero = jnp.zeros((), jnp.float32)
+        return [
+            [
+                jnp.where(low, plain, zero).astype(jnp.bfloat16),
+                jnp.where(low, zero, other).astype(jnp.bfloat16),
+            ],
+            [
+                jnp.where(low, other, zero).astype(jnp.bfloat16),
+                jnp.where(low, zero, plain).astype(jnp.bfloat16),
+            ],
+        ]
+
+    keys, values = spread(q_cols), spread(q_cols + k_cols)
+    norm_rows = log_norm[...].T
+    for part in range(moe_parts):
+        resid_gather.relay(part)
+    for part in range(moe_parts):
+        resid_gather.arrived(part)
+    for part in range(local_experts):
+        downs.fold(part)
+    at_lane = lax.broadcasted_iota(jnp.int32, (1, 128), 1)
+    for block in range(shards):
+        here = pl.ds(block * token_rows, token_rows)
+        grads = outer_cols(all_resid[block], full_out).astype(jnp.bfloat16)
+        head_grads[here, :] = grads
+        products = to_f32(grads) * heads_out[here, :]
+        deltas = jnp.zeros((token_rows, 128), jnp.float32)
+        for pair in range(2):
+            both = products[:, pair * 128 : pair * 128 + 128]
+            first = jnp.sum(jnp.where(low, both, 0.0), -1, keepdims=True)
+            second = jnp.sum(jnp.where(low, 0.0, both), -1, keepdims=True)
+            deltas = jnp.where(at_lane == 2 * pair, first, deltas)
+            deltas = jnp.where(at_lane == 2 * pair + 1, second, deltas)
+        turned[:, here] = deltas.T
+    attn_low = heads_out[...].astype(jnp.bfloat16)
+    flat_resid = all_resid[...].reshape(shards * token_rows, width)
+    out_grads[...] = (
+        inner_rows(attn_low, flat_resid).astype(jnp.bfloat16).reshape(groups, rows, width)
+    )
+    out_scatter = ExpScatter(
+        place,
+        lambda line, part: out_grads.at[line * 2 + 1 - place.x],
+        lambda line, part: out_grads.at[line * 2 + place.x],
+        lambda line, part: out_crossed.at[line],
+        lambda line, part: out_raised.at[raised_slot(line)],
+        lambda line, part: out_lowered.at[lowered_slot(line)],
+        1,
+        (out_xs, out_xr, out_ls, out_lr),
+    )
+    for line in order:
+        out_scatter.begin(line, 0)
+    key_grads[...] = jnp.zeros_like(key_grads)
+    value_grads[...] = jnp.zeros_like(value_grads)
+    for block in range(shards):
+        here = pl.ds(block * token_rows, token_rows)
+        count = (block + 1) * token_rows
+        at_col = block * token_rows + lax.broadcasted_iota(jnp.int32, (1, token_rows), 1)
+        at_row = lax.broadcasted_iota(jnp.int32, (count, 1), 0)
+        bias = jnp.where(
+            (at_row <= at_col) & (seg_col[:count, :] == seg_row[:, here]), 0.0, MASK_FILLER
+        )
+        for pair in range(2):
+            lanes = slice(pair * 128, pair * 128 + 128)
+            queries = qkv[here, lanes]
+            grads = head_grads[here, lanes]
+            query_grad = jnp.zeros((token_rows, 128), jnp.float32)
+            for head in range(2):
+                row = 2 * pair + head
+                mine = low if head == 0 else jnp.logical_not(low)
+                own_queries = jnp.where(mine, queries, jnp.zeros((), jnp.bfloat16))
+                own_grads = jnp.where(mine, grads, jnp.zeros((), jnp.bfloat16))
+                key, value = keys[pair][head][:count], values[pair][head][:count]
+                scores = outer_cols(key, queries) * factor + bias
+                probs = jnp.exp(scores - norm_rows[row : row + 1, block * token_rows : count])
+                grad_probs = outer_cols(value, grads)
+                grad_scores = (probs * (grad_probs - turned[row : row + 1, here])).astype(
+                    jnp.bfloat16
+                )
+                value_grads[pair, :count, :] += dot_rows(probs.astype(jnp.bfloat16), own_grads)
+                key_grads[pair, :count, :] += dot_rows(grad_scores, own_queries)
+                query_grad = query_grad + inner_rows(grad_scores, key)
+            qkv_grads[here, lanes] = (query_grad * factor).astype(jnp.bfloat16)
+        if block == 0:
+            for line in order:
+                out_scatter.fold(line, 0)
+        if block == 1:
+            for part in range(mix_parts):
+                mix.fold(3, part)
+                mix.fold(0, part)
+        if block == 2:
+            for part in range(mix_parts):
+                mix.fold(2, part)
+                mix.fold(1, part)
+
+    def fold_heads(first, second):
+        return jnp.where(
+            low,
+            first + pltpu.roll(first, HEAD_SIZE, 1),
+            second + pltpu.roll(second, HEAD_SIZE, 1),
+        )
+
+    qkv_grads[:, q_cols : q_cols + k_cols] = (
+        fold_heads(key_grads[0], key_grads[1]) * factor
+    ).astype(jnp.bfloat16)
+    qkv_grads[:, q_cols + k_cols :] = fold_heads(value_grads[0], value_grads[1]).astype(
+        jnp.bfloat16
+    )
+
+    token_load.wait()
+    normed_scatter = CtxScatter(
+        place,
+        lambda y, part: normed_part.at[2 * y + 1 - place.half],
+        lambda y, part: normed_part.at[2 * y + place.half],
+        lambda lane, part: moe_raised.at[lane],
+        lambda part: moe_raised.at[2],
+        1,
+        normed_send,
+        normed_recv,
+    )
+    gain_one_sum = jnp.zeros((1, width), jnp.float32)
+    main_sum = jnp.zeros((width, main_cols), jnp.float32)
+    for block in range(shards):
+        here = pl.ds(block * token_rows, token_rows)
+        grads = outer_cols(qkv_grads[here, :], full[:, :main_cols])
+        normed_part[block] = grads.astype(jnp.bfloat16)
+        own = to_f32(token_blocks[block])
+        scaled = own * rms_scale(own)
+        gain_one_sum = gain_one_sum + jnp.sum(grads * scaled, 0, keepdims=True)
+        normed = (scaled * gain_one_row).astype(jnp.bfloat16)
+        main_sum = main_sum + inner_rows(normed, qkv_grads[here, :])
+    normed_scatter.swap(False, 0).start()
+    normed_scatter.swap(True, 0).start()
+    at_sub = lax.broadcasted_iota(jnp.int32, (128, 1), 0)
+    gain_rows = jnp.where(
+        at_sub == EXPERTS, gain_one_sum, jnp.where(at_sub == EXPERTS + 1, gain_two_sum, 0.0)
+    )
+    side = router_sum[...] + gain_rows.T
+    sums[:, :, :, :main_cols] = main_sum.astype(jnp.bfloat16).reshape(
+        shards, groups, rows, main_cols
+    )
+    sums[:, :, :, main_cols:] = side.astype(jnp.bfloat16).reshape(
+        shards, groups, rows, pack_cols - main_cols
+    )
+    sum_scatter = ExpScatter(
+        place,
+        lambda line, part: sums.at[:, line * 2 + 1 - place.x],
+        lambda line, part: sums.at[:, line * 2 + place.x],
+        lambda line, part: sums_crossed.at[line],
+        lambda line, part: sums_raised.at[raised_slot(line)],
+        lambda line, part: sums_lowered.at[lowered_slot(line)],
+        1,
+        (sum_xs, sum_xr, sum_ls, sum_lr),
+    )
+    for line in order:
+        sum_scatter.begin(line, 0)
+    normed_scatter.fold(0)
+    for part in range(mix_parts):
+        size = token_rows // mix_parts
+        here = pl.ds(part * size, size)
+        mixed_out[here, :] = (resid[here, :] + mix.total(part)).astype(jnp.bfloat16)
+    output_sum[...] = out_scatter.total(0)
+    for line in order:
+        sum_scatter.fold(line, 0)
+    stores = []
+    for part in range(local_experts):
+        slot = part % 2
+        if part >= 2:
+            for copy in stores[2 * (part - 2) : 2 * (part - 1)]:
+                copy.wait()
+        in_stage[slot] = into.total(part)
+        down_stage[slot] = downs.total(part)
+        for kind, (source, target) in enumerate(
+            ((in_stage.at[slot], in_sum.at[part]), (down_stage.at[slot], down_sum.at[part]))
+        ):
+            copy = pltpu.make_async_copy(source, target, store_sem.at[kind, part])
+            copy.start()
+            stores.append(copy)
+    sums_own[...] = sum_scatter.total(0).astype(jnp.bfloat16)
+    sums_all[ctx] = sums_own[ctx]
+    copies = []
+    for lane, to in enumerate((place.core, place.side, place.far)):
+        copy = remote(
+            sums_own.at[to[0]], sums_all.at[ctx], last_send.at[lane], last_recv.at[lane], to
+        )
+        copy.start()
+        copies.append(copy)
+    grad_normed = normed_scatter.total(0)
+    own = to_f32(tokens[...])
+    scale = rms_scale(own)
+    weighted = grad_normed * gain_one_row
+    grad_tokens[...] = (
+        grad_resid[...]
+        + scale * weighted
+        - own * (scale * scale * scale) * jnp.mean(weighted * own, -1, keepdims=True)
+    )
+    for lane, to in enumerate((place.core, place.side, place.far)):
+        remote(
+            sums_own.at[0], sums_all.at[to[0]], last_send.at[lane], last_recv.at[lane], to
+        ).wait_recv()
+    side = jnp.zeros((rows, pack_cols - main_cols), jnp.float32)
+    for shard in range(shards):
+        came = to_f32(sums_all[shard])
+        query_sum[:, shard * q_cols : (shard + 1) * q_cols] = came[:, :q_cols]
+        key_sum[:, shard * k_cols : (shard + 1) * k_cols] = came[:, q_cols : q_cols + k_cols]
+        value_sum[:, shard * k_cols : (shard + 1) * k_cols] = came[:, q_cols + k_cols : main_cols]
+        side = side + came[:, main_cols:]
+    side_sum[...] = side
+    for copy in stores[-4:]:
+        copy.wait()
+    for copy in copies:
+        copy.wait_send()
+    for scatter in (mix, into, downs, out_scatter, normed_scatter, sum_scatter):
+        scatter.finish()
+    for part in range(moe_parts):
+        resid_gather.sent(part)
+
+
+def back(
+    moe_part, mixed_part, grad_in, grad_down, tokens, cot, resid, gain_two, gain_one, router_sum,
+    all_tokens, weights, out_rows, qkv, heads_out, log_norm, seg_col, seg_row,
+):
+    token_rows, width = tokens.shape
+    shards, groups, rows, pack_cols = weights.shape
+    seq_len = shards * token_rows
+    q_cols, main_cols = heads_out.shape[1], qkv.shape[1]
+    k_cols = (main_cols - q_cols) // 2
+    experts, _, in_rows, in_cols = grad_in.shape
+    down_rows = grad_down.shape[2]
+    low, f32 = jnp.bfloat16, jnp.float32
+
+    def shape(dims, dtype):
+        return jax.ShapeDtypeStruct(dims, dtype)
+
+    whole, anywhere = pl.BlockSpec(memory_space=VMEM), pl.BlockSpec(memory_space=pl.ANY)
+    block, steps = (LINES, token_rows, width), (LINES - 1, token_rows, width)
+    pack = (shards, rows, pack_cols)
+    return pl.pallas_call(
+        back_kernel,
+        name="back",
+        out_shape=[
+            shape((token_rows, width), low),
+            shape((token_rows, width), f32),
+            shape((rows, shards * q_cols), f32),
+            shape((rows, shards * k_cols), f32),
+            shape((rows, shards * k_cols), f32),
+            shape((rows, pack_cols - main_cols), f32),
+            shape((rows, width), f32),
+            shape((experts, in_rows, in_cols), f32),
+            shape((experts, down_rows, width), f32),
+        ],
+        in_specs=[anywhere] * 4 + [whole] * 6 + [anywhere] + [whole] * 7,
+        out_specs=[whole] * 7 + [anywhere] * 2,
+        scratch_shapes=[
+            *[VMEM(block, low), VMEM(block, low), VMEM(steps, low), VMEM(steps, low)] * 2,
+            VMEM((2, experts, in_rows, in_cols), low),
+            VMEM((2, experts, in_rows, in_cols), low),
+            VMEM((experts, in_rows, in_cols), low),
+            VMEM((2, experts, down_rows, width), low),
+            VMEM((2, experts, down_rows, width), low),
+            VMEM((experts, down_rows, width), low),
+            VMEM((token_rows, width), f32),
+            VMEM((shards, token_rows, width), low),
+            VMEM((seq_len, q_cols), low),
+            VMEM((128, seq_len), f32),
+            VMEM((2, seq_len, 128), f32),
+            VMEM((2, seq_len, 128), f32),
+            VMEM((seq_len, main_cols), low),
+            VMEM((shards, groups, rows, pack_cols), low),
+            VMEM((LINES,) + pack, low),
+            *[VMEM((LINES - 1,) + pack, low)] * 2,
+            VMEM((shards, rows, pack_cols), low),
+            VMEM((shards, rows, pack_cols), low),
+            VMEM((groups, rows, width), low),
+            VMEM((LINES, rows, width), low),
+            *[VMEM((LINES - 1, rows, width), low)] * 2,
+            VMEM((2, in_rows, in_cols), f32),
+            VMEM((2, down_rows, width), f32),
+            DMA((2, experts)),
+            DMA((12,)),
+            DMA,
+            *scatter_sems(4),
+            *scatter_sems(2),
+            *scatter_sems(1),
+            *scatter_sems(1),
+            *square_sems(experts),
+            *square_sems(experts),
+            *square_sems(1),
+            *square_sems(4),
+            DMA((3,)),
+            DMA((3,)),
+        ],
+        compiler_params=pltpu.CompilerParams(
+            collective_id=1, has_side_effects=True, vmem_limit_bytes=62 * 2**20
+        ),
+    )(
+        moe_part, mixed_part, grad_in, grad_down, tokens, cot, resid, gain_two, gain_one, router_sum,
+        all_tokens, weights, out_rows, qkv, heads_out, log_norm, seg_col, seg_row,
+    )
+
+
+def softmax_members(logits, member):
+    top = jnp.max(jnp.where(member, logits, MASK_FILLER), -1, keepdims=True)
+    weights = jnp.where(member, jnp.exp(logits - top), 0.0)
+    return weights / jnp.sum(weights, -1, keepdims=True)
+
+
+def two_parts(values):
+    high = values.astype(jnp.bfloat16)
+    return high, (values - high.astype(jnp.float32)).astype(jnp.bfloat16)
+
+
+def by_heads(
+    tokens,
+    segments,
+    routes,
+    gain_attn,
+    gain_moe,
+    query_weight,
+    key_weight,
+    value_weight,
+    w_output,
+    w_router,
+    w_expert_in,
+    w_expert_out,
+    cotangent,
+):
+    shards = lax.axis_size("ctx")
+    groups = lax.axis_size("exp")
+    exp_rank = lax.axis_index("exp")
+    local_experts = EXPERTS // groups
+    token_rows, width = tokens.shape[1], tokens.shape[2]
+    rows = query_weight.shape[0]
+    q_cols = query_weight.shape[1] // shards
+    k_cols = key_weight.shape[1] // shards
+    main_cols = q_cols + 2 * k_cols
+    side = 128
+
+    side_cols = jnp.concatenate(
+        [
+            w_router,
+            gain_attn[:, None],
+            gain_moe[:, None],
+            jnp.zeros((rows, side - EXPERTS - 2), jnp.bfloat16),
+        ],
+        1,
+    )
+    seg_col, seg_row = segments[0][:, None], segments
+    (
+        all_moe,
+        all_cot,
+        all_routes,
+        all_in,
+        all_out,
+        all_tokens,
+        all_weights,
+        out_rows,
+        qkv,
+        heads_out,
+        log_norm,
+        resid,
+    ) = front(
+        tokens[0],
+        side_cols,
+        query_weight,
+        key_weight,
+        value_weight,
+        w_output,
+        routes[0].T,
+        seg_col,
+        seg_row,
+        cotangent[0],
+        w_expert_in,
+        w_expert_out,
+    )
+    expert_in = all_in.reshape(local_experts, width, -1)
+    expert_out = all_out.reshape(local_experts, FF, -1)
+    side_rows = all_weights[..., main_cols:].reshape(width, side)
+    router = side_rows[:, :EXPERTS]
+    gains = side_rows[:, EXPERTS : EXPERTS + 2].astype(jnp.float32).T
+
+    member = jnp.any(
+        all_routes[..., None] == jnp.arange(EXPERTS, dtype=jnp.int32), axis=1
+    )
+    logits = jnp.einsum("std,de->ste", all_moe, router, preferred_element_type=jnp.float32)
+    gates = softmax_members(logits, member)
+    earlier = jnp.tril(jnp.ones((token_rows, token_rows), jnp.bfloat16), -1)
+    rank = jnp.einsum(
+        "tu,sue->ste", earlier, member.astype(jnp.bfloat16), preferred_element_type=jnp.float32
+    ).astype(jnp.int32)
+    kept = member & (rank < CAP)
+    first = exp_rank * local_experts
+
+    def mine(table):
+        return lax.dynamic_slice_in_dim(table, first, local_experts, 2)
+
+    place = jnp.where(mine(kept), mine(rank), -1)
+    pick = (
+        place.transpose(0, 2, 1)[:, :, None, :]
+        == jnp.arange(CAP, dtype=jnp.int32)[None, None, :, None]
+    ).astype(jnp.bfloat16)
+    both = jnp.concatenate([all_moe, all_cot], -1)
+    slots = jnp.einsum("sjct,std->sjcd", pick, both, preferred_element_type=jnp.float32)
+    slot_rows = slots[..., :width].astype(jnp.bfloat16)
+    slot_cot = slots[..., width:]
+    slot_gate = jnp.sum(
+        pick.astype(jnp.float32) * mine(gates).transpose(0, 2, 1)[:, :, None, :], -1
+    )
+    pre = jnp.einsum("sjcd,jdf->sjcf", slot_rows, expert_in, preferred_element_type=jnp.float32)
+    gate_part, up_part = pre[..., :FF], pre[..., FF:]
+    sigmoid_gate = jax.nn.sigmoid(gate_part)
+    hidden = (gate_part * sigmoid_gate * up_part).astype(jnp.bfloat16)
+    expert_rows = jnp.einsum(
+        "sjcf,jfd->sjcd", hidden, expert_out, preferred_element_type=jnp.float32
+    ).astype(jnp.bfloat16)
+    weighted = (slot_gate[..., None] * expert_rows.astype(jnp.float32)).astype(jnp.bfloat16)
+    mixed_part = jnp.einsum(
+        "sjct,sjcd->std", pick, weighted, preferred_element_type=jnp.float32
+    ).astype(jnp.bfloat16)
+    grad_rows = (slot_gate[..., None] * slot_cot).astype(jnp.bfloat16)
+    slot_dot = jnp.sum(slot_cot * expert_rows.astype(jnp.float32), -1)
+    grad_picked = jnp.sum(pick.astype(jnp.float32) * slot_dot[..., None], 2).transpose(0, 2, 1)
+    grad_picked = lax.dynamic_update_slice_in_dim(jnp.zeros_like(gates), grad_picked, first, 2)
+    grad_logits = gates * (grad_picked - jnp.sum(gates * grad_picked, -1, keepdims=True))
+    logits_high, logits_low = two_parts(grad_logits)
+    grad_router = jnp.einsum(
+        "std,ste->de", all_moe, logits_high, preferred_element_type=jnp.float32
+    ) + jnp.einsum("std,ste->de", all_moe, logits_low, preferred_element_type=jnp.float32)
+    grad_hidden = jnp.einsum(
+        "sjcd,jfd->sjcf", grad_rows, expert_out, preferred_element_type=jnp.float32
+    )
+    grad_gate = grad_hidden * up_part * sigmoid_gate * (1.0 + gate_part * (1.0 - sigmoid_gate))
+    grad_up = grad_hidden * gate_part * sigmoid_gate
+    grad_pre = jnp.concatenate([grad_gate, grad_up], -1).astype(jnp.bfloat16)
+    grad_slots = jnp.einsum(
+        "sjcf,jdf->sjcd", grad_pre, expert_in, preferred_element_type=jnp.float32
+    ).astype(jnp.bfloat16)
+    moe_part = (
+        jnp.einsum("sjct,sjcd->std", pick, grad_slots, preferred_element_type=jnp.float32)
+        + jnp.einsum("ste,de->std", logits_high, router, preferred_element_type=jnp.float32)
+        + jnp.einsum("ste,de->std", logits_low, router, preferred_element_type=jnp.float32)
+    ).astype(jnp.bfloat16)
+    grad_expert_out = jnp.einsum(
+        "sjcf,sjcd->jfd", hidden, grad_rows, preferred_element_type=jnp.float32
+    ).astype(jnp.bfloat16)
+    grad_expert_in = jnp.einsum(
+        "sjcd,sjcf->jdf", slot_rows, grad_pre, preferred_element_type=jnp.float32
+    ).astype(jnp.bfloat16)
+
+    router_sum = jnp.pad(grad_router, ((0, 0), (0, side - EXPERTS)))
+    (
+        mixed_out,
+        grad_tokens,
+        query_sum,
+        key_sum,
+        value_sum,
+        side_sum,
+        output_sum,
+        in_sum,
+        down_sum,
+    ) = back(
+        moe_part,
+        mixed_part,
+        grad_expert_in.reshape(all_in.shape),
+        grad_expert_out.reshape(all_out.shape),
+        tokens[0],
+        cotangent[0],
+        resid,
+        gains[1:2],
+        gains[0:1],
+        router_sum,
+        all_tokens,
+        all_weights,
+        out_rows,
+        qkv,
+        heads_out,
+        log_norm,
+        seg_col,
+        seg_row,
+    )
+    return (
+        mixed_out[None],
+        grad_tokens[None],
+        side_sum[:, EXPERTS],
+        side_sum[:, EXPERTS + 1],
+        query_sum,
+        key_sum,
+        value_sum,
+        output_sum,
+        side_sum[:, :EXPERTS],
+        in_sum,
+        down_sum,
+    )
+
+
 def solution(mesh):
+    sizes = (mesh.shape["ctx"], mesh.shape["exp"])
     return jax.shard_map(
-        local,
+        by_heads if sizes == (4, 8) else local,
         mesh=mesh,
         in_specs=(
             P("exp", "ctx", None),

time: 1800 us -> 546 us (0.30)
  waiting for transfers between devices: 1150 us -> 0 us
  Pallas kernels: 0 us -> 409 us
  blocking collectives: 340 us -> 0 us
  local copies, waits for them, and re-layouts: 86.7 us -> 27.7 us
  other arithmetic: 60.9 us -> 8.87 us
  matrix products: 128 us -> 90.3 us
    reduce_scatter x8 -> x0, waiting for transfers between devices: 761 us -> none  [the longest x1 143 us: local(): lax.psum_scatter(grad_output_w, ('ctx', 'exp'), scatter_dimension=0, tile...]
    pallas_call x0 -> x2, Pallas kernels: none -> 409 us  [the longest x1 233 us: front(): pl.pallas_call(front_kernel, name='front', out_shape=[shape((groups, toke...]
    all_to_all x3 -> x0, waiting for transfers between devices: 207 us -> none  [the longest x1 104 us: local(): lax.all_to_all(send_rows, 'exp', split_axis=0, concat_axis=0, tiled=True)]
    all_gather x8 -> x0, waiting for transfers between devices: 178 us -> none  [the longest x1 57.9 us: local(): lax.all_gather(query_weight, ('ctx', 'exp'), axis=0, tiled=True)]
    all_gather x1 -> x0, blocking collectives: 152 us -> none  [local(): lax.all_gather(w_router, ('ctx', 'exp'), axis=0, tiled=True)]
    all_to_all x1 -> x0, blocking collectives: 105 us -> none  [local(): lax.all_to_all(grad_send, 'exp', split_axis=0, concat_axis=0, tiled=True)]
    unnamed x2 -> x0, blocking collectives: 81.8 us -> none
    gather x5 -> x0, local copies, waits for them, and re-layouts: 56.5 us -> none  [the longest x1 14 us: local(): jnp.take(grad_back, safe_slot, axis=0)]
  transfers between devices with their start and end apart: 19 -> 0, of which waited for: 15 -> 0; matrix products, arithmetic and copies ran while one was open for 7% -> 0% of each run, Pallas kernels for 0% -> 0%
where the time goes in v2:
time: 546 us; the launch traced here: 537 us
  Pallas kernels  409 us (75%)
  matrix products  90.3 us (17%)
  local copies, waits for them, and re-layouts  27.7 us (5%)
  other arithmetic  8.87 us (2%)
    pallas_call x1, Pallas kernels, front(): pl.pallas_call(front_kernel, name='front', out_shape=[shape((groups, toke...  233 us
    pallas_call x1, Pallas kernels, back(): pl.pallas_call(back_kernel, name='back', out_shape=[shape((token_rows, wi...  176 us
    unnamed x24, local copies, waits for them, and re-layouts  19.3 us
    dot_general x1, matrix products, by_heads(): jnp.einsum('sjcd,sjcf->jdf', slot_rows, grad_pre, preferred_element_type=...  12.3 us

profile of v2, /device:TPU:0, one launch (start us, length us, event | category | flops | bytes accessed | tf_op | source)
XLA Modules:
  0.0 537.1 jit_solution(1230533850609290894)
XLA Ops:
  0.6 1.7 copy.63.seg_col
  2.4 0.7 copy.61
  3.1 0.8 copy.62
  3.9 0.1 pad.12.clone
  3.9 1.4 maximum_maximum_fusion.side_cols
  5.3 232.8 %front.1 = (bf16[8,256,1024]{2,1,0:T(8,128)(2,1)}, bf16[8,256,1024]{2,1,0:T(8,128)(2,1)}, s32[8,8,256]{2,1,0:T(8,128)}, bf16[4,4,256,1024]{3,2,1,0:T(8,128)(2,1)...) custom-call(bf16[256,1024]{1,0:T(8,128)(2,1)} %bitcast.121, ...), custom_call_target="tpu_custom_call" | custom-call | tf_op jit(solution)/shard_map/front/pallas_call | solution.py:965
  238.1 1.1 fusion.39
  239.2 0.3 convolution_convert_fusion.1
  239.6 10.3 %fusion.3 = f32[8,4,72,2048]{3,2,1,0:T(8,128)} fusion(bf16[8,256,1024]{2,1,0:T(8,128)(2,1)} %get-tuple-element.37, bf16[8,256,1024]{2,1,0:T(8,128)(2,1)} %get-tuple-element.35, s32[8,4,256]{2,1,0:T(4,128)S(1)} %fusion.58), kind=kOutput, calls=%fused_computation.9 | convolution fusion | flops 2433286144 | bytes 27295744 | tf_op jit(solution)/shard_map/sjct,std->sjcd/dot_general | solution.py:1634
  250.0 9.8 %fusion.28 = f32[8,4,72,1024]{3,2,0,1:T(8,128)S(1)} fusion(bf16[4,1024,1024,1]{2,1,3,0:T(8,128)(2,1)} %bitcast.133, f32[8,4,72,2048]{3,2,1,0:T(8,128)} %fusion.3), kind=kOutput, calls=%fused_computation.41 | convolution fusion | flops 4831838208 | bytes 22544384 | tf_op jit(solution)/shard_map/sjcd,jdf->sjcf/dot_general | solution.py:1640
  259.8 3.3 multiply_convert_fusion.1
  263.0 1.3 copy-done.1
  264.3 10.5 %fusion.1 = (f32[8,4,72]{2,1,0:T(4,128)S(1)}, bf16[4,1024,8,72]{1,3,0,2:T(8,128)(2,1)}) fusion(f32[8,4,72,2048]{3,2,1,0:T(8,128)} %fusion.3, bf16[4,512,1024,1]{2,1,0,3:T(8,128)(2,1)} %bitcast.135, bf16[8,4,72,512]{3,2,0,1:T(8,128)(2,1)} %multiply_convert_fusion.1), kind=kOutput, calls=%fused_computation.5 | convolution fusion | flops 2425353984 | bytes 20718592 | tf_op jit(solution)/shard_map/sjcf,jfd->sjcd/dot_general | solution.py:1644
  274.8 1.0 slice.37
  275.8 1.3 fusion.50
  277.2 1.1 fusion.65
  278.3 1.7 fusion.35
  280.0 0.1 multiply_reduce_fusion
  280.1 0.1 subtract_convert_fusion
  280.1 0.0 copy-start.2
  280.2 0.8 convolution_bitcast_fusion
  281.0 1.5 fusion.46
  282.5 1.1 copy.72
  283.6 0.8 pad.4.router_sum
  284.5 0.0 copy-done.2
  284.5 9.3 %bitcast_convert_fusion.1 = bf16[4,512,1024]{2,1,0:T(8,128)(2,1)} fusion(bf16[8,4,72,512]{3,2,0,1:T(8,128)(2,1)S(1)} %copy-done.2, f32[8,4,72,2048]{3,2,1,0:T(8,128)} %fusion.3, f32[8,4,72]{2,1,0:T(4,128)S(1)} %get-tuple-element.53), kind=kOutput, calls=%fused_computation.12 | convolution fusion | flops 2422734848 | bytes 16000000 | tf_op jit(solution)/shard_map/sjcf,sjcd->jfd/dot_general | solution.py:1674
  293.7 0.0 copy-done.4
  293.7 9.9 %fusion.14 = (bf16[8,4,72,512]{3,2,0,1:T(8,128)(2,1)S(1)}, bf16[8,4,72,512]{3,2,0,1:T(8,128)(2,1)}) fusion(f32[8,4,72,1024]{3,2,0,1:T(8,128)} %copy-done.1, bf16[4,512,1024,1]{2,1,3,0:T(8,128)(2,1)S(1)} %bitcast.136, f32[8,4,72,2048]{3,2,1,0:T(8,128)} %fusion.3, f32[8,4,72]{2,1,0:T(4,128)S(1)} %get-tuple-element.53), kind=kOutput, calls=%fused_computation.25 | convolution fusion | flops 2435973120 | bytes 27796480 | tf_op jit(solution)/shard_map/sjcd,jfd->sjcf/dot_general | solution.py:1660
  303.6 12.3 %bitcast_convert_fusion = bf16[4,1024,1024]{2,1,0:T(8,128)(2,1)} fusion(f32[8,4,72,2048]{3,2,1,0:T(8,128)} %fusion.3, bf16[8,4,72,512]{3,2,0,1:T(8,128)(2,1)} %get-tuple-element.60, bf16[8,4,72,512]{3,2,0,1:T(8,128)(2,1)S(1)} %get-tuple-element.59), kind=kOutput, calls=%fused_computation.1 | convolution fusion | flops 4845469696 | bytes 17825792 | tf_op jit(solution)/shard_map/sjcd,sjcf->jdf/dot_general | solution.py:1677
  315.9 4.6 bitcast_convert_fusion.2.mixed_part
  320.5 10.4 %fusion.22 = bf16[4,1024,8,72]{1,3,0,2:T(8,128)(2,1)} fusion(bf16[4,1024,1024,1]{2,1,0,3:T(8,128)(2,1)} %bitcast.134, bf16[8,4,72,512]{3,2,0,1:T(8,128)(2,1)} %get-tuple-element.60, bf16[8,4,72,512]{3,2,0,1:T(8,128)(2,1)S(1)} %get-tuple-element.59), kind=kOutput, calls=%fused_computation.35 | convolution fusion | flops 4841275392 | bytes 17825792 | tf_op jit(solution)/shard_map/sjcf,jdf->sjcd/dot_general | solution.py:1666
  330.9 4.7 fusion.10
  335.6 1.3 fusion.49
  336.9 3.3 fusion.7.moe_part
  340.2 0.1 slice_convert_fusion.1
  340.3 0.2 copy.84
  340.5 0.6 fusion.64
  341.1 176.2 %back.1 = (bf16[256,1024]{1,0:T(8,128)(2,1)}, f32[256,1024]{1,0:T(8,128)}, f32[32,1024]{1,0:T(8,128)}, f32[32,512]{1,0:T(8,128)}, f32[32,512]{1,0:T(8,128)}, /*i...) custom-call(bf16[8,256,1024]{2,1,0:T(8,128)(2,1)} %fusion.7.moe_part, ...), custom_call_target="tpu_custom_call" | custom-call | tf_op jit(solution)/shard_map/back/pallas_call | solution.py:1469
  517.3 1.5 slice_reduce_fusion
  518.8 1.9 copy.115
  520.7 2.3 copy.116
  523.0 1.7 copy.117
  524.7 1.5 copy.118
  526.2 1.5 copy.119
  527.7 1.6 copy.120
  529.2 1.3 copy.121
  530.5 4.8 copy.122
  535.3 1.3 copy.123
  (19 shorter events, 0.2 us)
Async XLA Ops:
  259.8 4.6 copy-start.1
  264.3 11.5 %copy-start = (bf16[8,256,1024]{2,1,0:T(8,128)(2,1)S(1)}, bf16[8,256,1024]{2,1,0:T(8,128)(2,1)}, u32[]{:S(2)}) copy-start(bf16[8,256,1024]{2,1,0:T(8,128)(2,1)} %get-tuple-element.35) | copy-start | bytes 12582916
  280.1 4.3 copy-start.2
  284.5 9.3 %copy-start.4 = (bf16[4,4,128,1024]{3,2,1,0:T(8,128)(2,1)S(1)}, bf16[4,4,128,1024]{3,2,1,0:T(8,128)(2,1)}, u32[]{:S(2)}) copy-start(bf16[4,4,128,1024]{3,2,1,0:T(8,128)(2,1)} %get-tuple-element.34) | copy-start | bytes 12582916
  293.7 22.1 %slice-start = ((s8[4718592]{0:T(1024)(128)(4,1)}), s8[524288]{0:T(1024)(128)(4,1)S(1)}, s32[]{:S(2)}) async-start(s8[4718592]{0:T(1024)(128)(4,1)} %bitcast.137), calls=%async_computation | async-start | bytes 1048576
  303.6 12.3 %slice-start.1 = ((s8[4718592]{0:T(1024)(128)(4,1)}), s8[4194304]{0:T(1024)(128)(4,1)S(1)}, s32[]{:S(2)}) async-start(s8[4718592]{0:T(1024)(128)(4,1)} %bitcast.137), calls=%async_computation.1 | async-start | bytes 8388608
  523.0 12.3 %copy-start.3 = (f32[4,128,1024]{2,1,0:T(8,128)S(1)}, f32[4,128,1024]{2,1,0:T(8,128)}, u32[]{:S(2)}) copy-start(f32[4,128,1024]{2,1,0:T(8,128)} %get-tuple-element.88) | copy-start | bytes 6291460
